TPU v7x, 256 devices: a whole 4x4x8 slice. The times are simulated.
256 devices in a mesh: dp: 16 (over x, y_hi, core), seq: 16 (over z, y_lo).
Axes of the slice: x: 4, y: 4 (y_hi: 2, y_lo: 2; y = y_hi * 2 + y_lo), z: 8, core: 2. Of those that a mesh axis runs over, the one named last changes fastest.
Arguments:
- coarse: bfloat16 [16, 4096, 1024], P('dp', 'seq'), may hold values from -6 to 6
- skip: bfloat16 [16, 8192, 768], P('dp', 'seq'), may hold values from -6 to 6
- conv_weight: bfloat16 [5, 1024, 768], replicated, may hold values from -0.078125 to 0.078125
- donor_weight: bfloat16 [768, 768], replicated, may hold values from -0.21875 to 0.21875
- acceptor_weight: bfloat16 [768, 768], replicated, may hold values from -0.21875 to 0.21875
- other_grad: bfloat16 [16, 8192, 768], P('dp', 'seq'), may hold values from -4 to 4
- score_grad: float32 [16, 1024], P('dp', 'seq'), may hold values from -16 to 16
- donor_pos: int32 [16, 1024], P('dp', 'seq'), may hold values from 0 to 511
- acceptor_pos: int32 [16, 1024], P('dp', 'seq'), may hold values from 0 to 8191, as said below
- pair_mask: int32 [16, 1024], P('dp', 'seq'), may hold values 0 or 1
Outputs:
- scores: float32 [16, 1024], P('dp', 'seq')
- coarse_grad: bfloat16 [16, 4096, 1024], P('dp', 'seq')
- donor_weight_grad: float32 [768, 768], P('seq')
- acceptor_weight_grad: float32 [768, 768], P('seq')
Inputs may be any that keep to these rules, and one draw needn't show every extreme that they name: Position in the whole sample. Among the 64 slots held by one shard of a sample, at most 8 have their acceptor on any one shard (shard = acceptor_pos // 512); in every sample some shard is named by exactly 8 slots of every shard.
All inputs are finite; a program needn't handle non-finite values. No bound on the sum of `pair_mask` on one device may be relied on, other than what follows from the above.
Results may differ from a plain program's by a relative error of at most 0.013.
Values may be sent and summed in bfloat16 or wider, within the bound.
A program may use at most 128 MiB of HBM per device.

v0:
```python
import math

import jax
import jax.numpy as jnp
from jax import lax
from jax.sharding import PartitionSpec as P

ACAP = 8


def with_halo(cells, sides, width):
    for axis, dim in sides:
        count = lax.axis_size(axis)
        ends = count - 1
        head = lax.slice_in_dim(cells, 0, width, axis=dim)
        tail = lax.slice_in_dim(cells, cells.shape[dim] - width, cells.shape[dim], axis=dim)
        cells = jnp.concatenate(
            [
                lax.ppermute(tail, axis, [(i, (i + 1) % count) for i in range(ends)]),
                cells,
                lax.ppermute(head, axis, [((i + 1) % count, i) for i in range(ends)]),
            ],
            axis=dim,
        )
    return cells


def activate(values):
    return jax.nn.gelu(values, approximate=True)


def on_device(
    coarse,
    skip,
    conv_weight,
    donor_weight,
    acceptor_weight,
    other_grad,
    score_grad,
    donor_pos,
    acceptor_pos,
    pair_mask,
):
    seq_count = lax.axis_size("seq")
    batch_count = lax.axis_size("dp")
    taps = conv_weight.shape[0]
    emb_width = donor_weight.shape[1]
    inverse_root = 1.0 / math.sqrt(emb_width)
    widened = with_halo(coarse, (("seq", 1),), 1)
    upsampled = jnp.repeat(widened[0], 2, axis=0)
    row_count = upsampled.shape[0] - 4
    preact = skip[0].astype(jnp.float32)
    for shift_index in range(taps):
        preact = preact + jnp.dot(
            upsampled[shift_index : shift_index + row_count],
            conv_weight[shift_index],
            preferred_element_type=jnp.float32,
        )
    activated = activate(preact).astype(jnp.bfloat16)
    donor_rows = donor_pos[0]
    donor_act = activated[donor_rows]
    donor_emb = jnp.dot(donor_act, donor_weight, preferred_element_type=jnp.float32).astype(
        jnp.bfloat16
    )
    targets = acceptor_pos[0]
    owner = targets // row_count
    local_row = targets % row_count
    owner_hits = (owner[:, None] == jnp.arange(seq_count, dtype=jnp.int32)[None, :]).astype(
        jnp.int32
    )
    place_rank = jnp.sum((jnp.cumsum(owner_hits, axis=0) - owner_hits) * owner_hits, axis=1)
    capacity = ACAP
    slot_index = owner * capacity + place_rank
    requests = (
        jnp.zeros((seq_count * capacity,), jnp.int32)
        .at[slot_index]
        .set(local_row)
        .reshape(seq_count, capacity)
    )
    received = lax.all_to_all(requests, "seq", split_axis=0, concat_axis=0, tiled=True)
    wanted = activated[received.reshape(-1)]
    projected = jnp.dot(wanted, acceptor_weight, preferred_element_type=jnp.float32).astype(
        jnp.bfloat16
    )
    projected = projected.reshape(received.shape[0], received.shape[1], emb_width)
    returned = lax.all_to_all(projected, "seq", split_axis=0, concat_axis=0, tiled=True)
    returned, served_rows = (returned, received)
    acceptor_emb = returned.reshape(seq_count * capacity, emb_width)[slot_index]
    mask_float = pair_mask[0].astype(jnp.float32)
    scores = (
        mask_float
        * jnp.sum(donor_emb.astype(jnp.float32) * acceptor_emb.astype(jnp.float32), axis=1)
        * inverse_root
    )
    weighted = score_grad[0] * mask_float
    donor_emb_grad = (weighted[:, None] * acceptor_emb.astype(jnp.float32) * inverse_root).astype(
        jnp.bfloat16
    )
    acceptor_emb_grad = (weighted[:, None] * donor_emb.astype(jnp.float32) * inverse_root).astype(
        jnp.bfloat16
    )
    outgoing = (
        jnp.zeros((seq_count * capacity, emb_width), jnp.bfloat16)
        .at[slot_index]
        .set(acceptor_emb_grad)
    )
    outgoing = outgoing.reshape(seq_count, capacity, emb_width)
    received = lax.all_to_all(outgoing, "seq", split_axis=0, concat_axis=0, tiled=True)
    flattened = received.reshape(-1, emb_width)
    to_rows = jnp.dot(flattened, acceptor_weight.T, preferred_element_type=jnp.float32)
    row_terms = to_rows.reshape(received.shape[0], received.shape[1], -1)
    served_flat = served_rows.reshape(-1)
    act_grad = other_grad[0].astype(jnp.float32)
    act_grad = act_grad.at[donor_rows].add(
        jnp.dot(donor_emb_grad, donor_weight.T, preferred_element_type=jnp.float32)
    )
    act_grad = act_grad.at[served_flat].add(row_terms.reshape(-1, row_terms.shape[2]))
    pull = jax.vjp(activate, preact)[1]
    preact_grad = pull(act_grad)[0].astype(jnp.bfloat16)
    widened_grad = with_halo(preact_grad[None], (("seq", 1),), 2)[0]
    upsampled_grad = jnp.zeros((row_count, conv_weight.shape[1]), jnp.float32)
    for shift_index in range(taps):
        begin = 4 - shift_index
        upsampled_grad = upsampled_grad + jnp.dot(
            widened_grad[begin : begin + row_count],
            conv_weight[shift_index].T,
            preferred_element_type=jnp.float32,
        )
    coarse_grad = (
        upsampled_grad.reshape(row_count // 2, 2, -1).sum(axis=1).astype(jnp.bfloat16)[None]
    )
    served_act = activated[served_flat]
    served_emb_grad = received.reshape(-1, emb_width)
    rows_each = donor_weight.shape[0] // seq_count
    factor = 1.0 / batch_count
    donor_term = jnp.dot(donor_act.T, donor_emb_grad, preferred_element_type=jnp.float32)
    acceptor_term = jnp.dot(served_act.T, served_emb_grad, preferred_element_type=jnp.float32)
    donor_total, acceptor_total = lax.psum((donor_term, acceptor_term), ("dp", "seq"))
    first_row = lax.axis_index("seq") * rows_each
    donor_part = lax.dynamic_slice_in_dim(donor_total, first_row, rows_each, 0)
    acceptor_part = lax.dynamic_slice_in_dim(acceptor_total, first_row, rows_each, 0)
    return (scores[None], coarse_grad, donor_part * factor, acceptor_part * factor)


def solution(mesh):
    in_specs = (
        P("dp", "seq", None),
        P("dp", "seq", None),
        P(),
        P(),
        P(),
        P("dp", "seq", None),
        P("dp", "seq"),
        P("dp", "seq"),
        P("dp", "seq"),
        P("dp", "seq"),
    )
    out_specs = (P("dp", "seq"), P("dp", "seq", None), P("seq", None), P("seq", None))
    return jax.shard_map(
        on_device, mesh=mesh, in_specs=in_specs, out_specs=out_specs, check_vma=False
    )
```

profile of v0, /device:TPU:1, one launch (start us, length us, event | category | flops | bytes accessed | tf_op | source)
XLA Modules:
  0.0 378.7 jit_solution(3904731837600903716)
XLA Ops:
  7.2 0.0 copy-start
  7.2 0.8 fusion.89
  8.0 4.0 %collective-permute-start = (bf16[1,1,1024]{2,1,0:T(2,128)(2,1)S(1)}, bf16[1,1,1024]{2,1,0:T(2,128)(2,1)S(1)}, u32[]{:S(2)}, u32[]{:S(2)}) collective-permute-start(bf16[1,1,1024]{2,1,0:T(2,128)(2,1)S(1)} %get-tuple-element.10), channel_id=1, source_target_pairs={{0,1},{1,2},{2,3},{3,4},{4,5},{5,6},{6,7},{7,8},{8,9},{9,10},{10,1... | collective-permute-start | bytes 6152 | tf_op jit(solution)/shard_map/ppermute | solution.py:19
  12.1 1.3 collective-permute-start.1
  13.4 0.7 and_select_fusion
  14.0 0.1 fusion.71
  14.1 0.1 reduce_window_sum.11
  14.2 0.2 select_reduce_fusion
  14.4 0.7 fusion.77
  15.1 0.8 scatter_custom_fusion
  15.8 0.7 all_to_all.12
  16.5 11.2 %all-to-all-start = ((s32[16,1,8]{2,1,0:T(1,128)}), s32[16,1,8]{2,1,0:T(1,128)S(1)}, u32[]{:S(2)}, u32[]{:S(2)}) async-start(s32[16,1,8]{2,1,0:T(1,128)} %bitcast.16), calls=%async_computation | async-start | bytes 16384 | tf_op jit(solution)/shard_map/all_to_all | solution.py:80
  27.7 1.6 broadcast_in_dim.14
  29.3 0.4 slice.107
  29.8 3.6 fusion.20
  33.4 1.6 all-to-all-done
  35.0 0.5 broadcast.232
  35.5 0.7 reduce.3
  36.2 0.1 reshape.228
  36.3 0.1 maximum_bitcast_fusion
  36.5 0.5 broadcast_in_dim.13
  37.0 1.4 reshape.227
  38.5 4.0 %fusion.16 = f32[512,768]{1,0:T(8,128)} fusion(bf16[5,1024,768]{2,1,0:T(8,128)(2,1)} %param.12, bf16[516,1024]{1,0:T(8,128)(2,1)} %reshape.227), kind=kOutput, calls=%fused_computation.27 | convolution fusion | flops 805306368 | bytes 4194304 | tf_op jit(solution)/shard_map/dot_general | solution.py:54
  42.4 3.6 fusion.24
  46.0 1.0 fusion.59
  47.0 0.5 broadcast_in_dim.15
  47.5 0.4 slice.113
  48.0 3.6 fusion.12
  51.6 0.5 broadcast_in_dim.12
  52.1 0.4 slice.101
  52.6 6.1 %multiply_convert_fusion = (bf16[512,768]{1,0:T(8,128)(2,1)S(1)}, f32[512,768]{1,0:T(8,128)}) fusion(f32[512,768]{1,0:T(8,128)} %fusion.12, f32[512,768]{1,0:T(8,128)} %fusion.16, f32[512,768]{1,0:T(8,128)} %fusion.20, f32[512,768]{1,0:T(8,128)} %fusion.24, bf16[512,1024]{1,0:T(8,128)(2,1)S(1)} %slice.101, bf16[5,1024,768]{2,1,0:T(8,128)(2,1)} %param.12, ...), kind=kOutput, calls=%fused_computation.41 | convolution fusion | flops 811204608 | bytes 12058624 | tf_op jit(solution)/shard_map/dot_general | solution.py:54
  58.7 0.9 gather_fusion.1
  59.5 1.0 fusion.40
  60.5 6.0 %all-to-all-start.1 = ((bf16[16,8,768]{2,1,0:T(8,128)(2,1)}), bf16[16,8,768]{2,1,0:T(8,128)(2,1)}, u32[]{:S(2)}, u32[]{:S(2)}) async-start(bf16[16,8,768]{2,1,0:T(8,128)(2,1)} %fusion.40), calls=%async_computation.1 | async-start | bytes 393216 | tf_op jit(solution)/shard_map/all_to_all | solution.py:86
  66.6 1.2 bitcast_convert_fusion
  67.9 1.3 gather_fusion
  69.2 6.5 %all-to-all-done.1 = bf16[16,8,768]{2,1,0:T(8,128)(2,1)} async-done(((bf16[16,8,768]{2,1,0:T(8,128)(2,1)}), bf16[16,8,768]{2,1,0:T(8,128)(2,1)}, u32[]{:S(2)}, u32[]{:S(2)}) %all-to-all-start.1) | async-done | bytes 196640 | tf_op jit(solution)/shard_map/all_to_all | solution.py:86
  75.7 1.7 gather_fusion.2
  77.4 1.8 fusion.60
  79.2 0.5 multiply_bitcast_fusion
  79.7 1.7 scatter_custom_fusion.2
  81.4 3.5 all-to-all-start.2
  85.0 0.2 all-reduce.3.cloned.1.call-start
  85.2 1.8 fusion.74
  87.0 0.0 copy-start.6
  87.0 1.6 scatter_fusion
  88.6 1.9 fusion.72
  90.5 3.5 all-to-all-done.2
  94.0 1.3 fusion.65
  95.3 2.5 scatter_fusion.1
  97.8 2.0 fusion.63
  99.8 0.0 all-reduce.3.cloned.1.call-update
  99.8 2.6 fusion.6
  102.4 1.6 collective-permute-start.2
  104.0 2.4 fusion.18
  106.4 4.0 %collective-permute-start.3 = (bf16[1,2,768]{2,1,0:T(2,128)(2,1)S(1)}, bf16[1,2,768]{2,1,0:T(2,128)(2,1)S(1)}, u32[]{:S(2)}, u32[]{:S(2)}) collective-permute-start(bf16[1,2,768]{2,1,0:T(2,128)(2,1)S(1)} %get-tuple-element.7), channel_id=1, source_target_pairs={{0,1},{1,2},{2,3},{3,4},{4,5},{5,6},{6,7},{7,8},{8,9},{9,10},{10,1... | collective-permute-start | bytes 9224 | tf_op jit(solution)/shard_map/ppermute | solution.py:19
  110.4 2.5 fusion.26
  113.0 1.0 fusion.22
  114.0 1.0 fusion.14
  115.1 2.4 add_add_fusion
  117.5 2.5 reshape.233
  120.0 3.6 reduce_sum.35
  123.5 246.7 %all-reduce.3.cloned.1.call-done = (f32[768,768]{1,0:T(8,128)}, f32[768,768]{1,0:T(8,128)}) async-done(((f32[768,768]{1,0:T(8,128)}, f32[768,768]{1,0:T(8,128)}), (f32[768,768]{1,0:T(8,128)}, f32[768,768]{1,0:T(8,128)})) %all-reduce.3.cloned.1.call-update) | async-done | bytes 4718608 | tf_op jit(solution)/shard_map/psum | solution.py:138
  370.2 1.7 dynamic-slice_multiply_fusion
  (35 shorter events, 0.1 us)
Async XLA Ops:
  7.2 52.4 %copy-start = (bf16[768,768]{1,0:T(8,128)(2,1)S(1)}, bf16[768,768]{1,0:T(8,128)(2,1)}, u32[]{:S(2)}) copy-start(bf16[768,768]{1,0:T(8,128)(2,1)} %param.14) | copy-start | bytes 3538948
  8.0 28.3 %collective-permute-start = (bf16[1,1,1024]{2,1,0:T(2,128)(2,1)S(1)}, bf16[1,1,1024]{2,1,0:T(2,128)(2,1)S(1)}, u32[]{:S(2)}, u32[]{:S(2)}) collective-permute-start(bf16[1,1,1024]{2,1,0:T(2,128)(2,1)S(1)} %get-tuple-element.10), channel_id=1, source_target_pairs={{0,1},{1,2},{2,3},{3,4},{4,5},{5,6},{6,7},{7,8},{8,9},{9,10},{10,1... | collective-permute-start | bytes 6152 | tf_op jit(solution)/shard_map/ppermute | solution.py:19
  12.1 24.3 %collective-permute-start.1 = (bf16[1,1,1024]{2,1,0:T(2,128)(2,1)S(1)}, bf16[1,1,1024]{2,1,0:T(2,128)(2,1)S(1)}, u32[]{:S(2)}, u32[]{:S(2)}) collective-permute-start(bf16[1,1,1024]{2,1,0:T(2,128)(2,1)S(1)} %get-tuple-element.11), channel_id=1, source_target_pairs={{1,0},{2,1},{3,2},{4,3},{5,4},{6,5},{7,6},{8,7},{9,8},{10,9},{11,1... | collective-permute-start | bytes 6152 | tf_op jit(solution)/shard_map/ppermute | solution.py:21
  15.1 18.4 %copy-start.9 = (s32[64]{0:T(128)}, s32[64]{0:T(128)S(1)}, u32[]{:S(2)}) copy-start(s32[64]{0:T(128)S(1)} %fusion.77) | copy-start | bytes 772
  16.5 18.5 %all-to-all-start = ((s32[16,1,8]{2,1,0:T(1,128)}), s32[16,1,8]{2,1,0:T(1,128)S(1)}, u32[]{:S(2)}, u32[]{:S(2)}) async-start(s32[16,1,8]{2,1,0:T(1,128)} %bitcast.16), calls=%async_computation | async-start | bytes 16384 | tf_op jit(solution)/shard_map/all_to_all | solution.py:80
  27.7 2.1 copy-start.10
  29.8 6.5 %copy-start.1 = (bf16[1,256,1024]{2,1,0:T(8,128)(2,1)S(1)}, bf16[1,256,1024]{2,1,0:T(8,128)(2,1)}, u32[]{:S(2)}) copy-start(bf16[1,256,1024]{2,1,0:T(8,128)(2,1)} %param.10) | copy-start | bytes 1572868
  38.5 4.0 %copy-start.5 = (bf16[516,1024]{1,0:T(8,128)(2,1)S(1)}, bf16[516,1024]{1,0:T(8,128)(2,1)}, u32[]{:S(2)}) copy-start(bf16[516,1024]{1,0:T(8,128)(2,1)} %reshape.227) | copy-start | bytes 3170308
  48.0 3.6 copy-start.2
  59.5 7.1 %copy-start.3 = (bf16[128,768]{1,0:T(8,128)(2,1)}, bf16[128,768]{1,0:T(8,128)(2,1)S(1)}, u32[]{:S(2)}) copy-start(bf16[128,768]{1,0:T(8,128)(2,1)S(1)} %gather_fusion.1) | copy-start | bytes 589828
  60.5 15.1 %all-to-all-start.1 = ((bf16[16,8,768]{2,1,0:T(8,128)(2,1)}), bf16[16,8,768]{2,1,0:T(8,128)(2,1)}, u32[]{:S(2)}, u32[]{:S(2)}) async-start(bf16[16,8,768]{2,1,0:T(8,128)(2,1)} %fusion.40), calls=%async_computation.1 | async-start | bytes 393216 | tf_op jit(solution)/shard_map/all_to_all | solution.py:86
  69.2 10.0 %copy-start.7 = (f32[1,64]{1,0:T(1,128)S(1)}, f32[1,64]{1,0:T(1,128)}, u32[]{:S(2)}) copy-start(f32[1,64]{1,0:T(1,128)} %param.16) | copy-start | bytes 772
  69.2 10.0 %copy-start.8 = (s32[1,64]{1,0:T(1,128)S(1)}, s32[1,64]{1,0:T(1,128)}, u32[]{:S(2)}) copy-start(s32[1,64]{1,0:T(1,128)} %param.19) | copy-start | bytes 772
  81.4 12.6 %all-to-all-start.2 = ((bf16[16,8,768]{2,1,0:T(8,128)(2,1)}), bf16[16,8,768]{2,1,0:T(8,128)(2,1)S(1)}, u32[]{:S(2)}, u32[]{:S(2)}) async-start(bf16[16,8,768]{2,1,0:T(8,128)(2,1)} %bitcast.23), calls=%async_computation.2 | async-start | bytes 393216 | tf_op jit(solution)/shard_map/all_to_all | solution.py:108
  85.0 285.2 %all-reduce.3.cloned.1.call-start = ((), (), s32[]{:S(2)}) async-start(), calls=%async_computation.3 | async-start | bytes 9437184 | tf_op jit(solution)/shard_map/psum | solution.py:138
  87.0 1.6 copy-start.6
  95.3 2.5 copy-start.4
  99.8 13.2 %slice-start = ((s8[7864320]{0:T(1024)(128)(4,1)}), s8[4194304]{0:T(1024)(128)(4,1)S(1)}, s32[]{:S(2)}) async-start(s8[7864320]{0:T(1024)(128)(4,1)} %bitcast.129), calls=%async_computation.4 | async-start | bytes 8388608
  102.4 10.6 %slice-start.1 = ((s8[7864320]{0:T(1024)(128)(4,1)}), s8[3670016]{0:T(1024)(128)(4,1)S(1)}, s32[]{:S(2)}) async-start(s8[7864320]{0:T(1024)(128)(4,1)} %bitcast.129), calls=%async_computation.5 | async-start | bytes 7340032
  102.4 8.0 %collective-permute-start.2 = (bf16[1,2,768]{2,1,0:T(2,128)(2,1)S(1)}, bf16[1,2,768]{2,1,0:T(2,128)(2,1)S(1)}, u32[]{:S(2)}, u32[]{:S(2)}) collective-permute-start(bf16[1,2,768]{2,1,0:T(2,128)(2,1)S(1)} %get-tuple-element.6), channel_id=1, source_target_pairs={{1,0},{2,1},{3,2},{4,3},{5,4},{6,5},{7,6},{8,7},{9,8},{10,9},{11,1... | collective-permute-start | bytes 9224 | tf_op jit(solution)/shard_map/ppermute | solution.py:21
  106.4 7.6 %collective-permute-start.3 = (bf16[1,2,768]{2,1,0:T(2,128)(2,1)S(1)}, bf16[1,2,768]{2,1,0:T(2,128)(2,1)S(1)}, u32[]{:S(2)}, u32[]{:S(2)}) collective-permute-start(bf16[1,2,768]{2,1,0:T(2,128)(2,1)S(1)} %get-tuple-element.7), channel_id=1, source_target_pairs={{0,1},{1,2},{2,3},{3,4},{4,5},{5,6},{6,7},{7,8},{8,9},{9,10},{10,1... | collective-permute-start | bytes 9224 | tf_op jit(solution)/shard_map/ppermute | solution.py:19
Sparse Core Ops, SparseCore 0:
  99.9 270.2 all-reduce.2
where the time goes:
time: 380 us; the launch traced here: 379 us
  waiting for transfers between devices  258 us (68%)
  matrix products  39.9 us (10%)
  starting transfers between devices  31.8 us (8%)
  other arithmetic  18.9 us (5%)
  local copies, waits for them, and re-layouts  15.4 us (4%)
  between operations  14.5 us (4%)
    psum x1, waiting for transfers between devices, on_device(): lax.psum((donor_term, acceptor_term), ('dp', 'seq'))  247 us
    dot_general x5, matrix products, on_device(): jnp.dot(upsampled[shift_index:shift_index + row_count], conv_weight[shift...  20.8 us
    all_to_all x1, starting transfers between devices, on_device(): lax.all_to_all(requests, 'seq', split_axis=0, concat_axis=0, tiled=True)  11.2 us
    dot_general x5, matrix products, on_device(): jnp.dot(widened_grad[begin:begin + row_count], conv_weight[shift_index].T...  9.4 us
    ppermute x2, starting transfers between devices, with_halo(): lax.ppermute(tail, axis, [(i, (i + 1) % count) for i in range(ends)])  8.01 us
  transfers between devices with their start and end apart: 8, of which 4 were waited for; matrix products, arithmetic and copies ran while one was open for 9% of the time, Pallas kernels for 0%

commit v1 on v0

v1 whole, which is shorter than its diff:
```python
import math

import jax
import jax.numpy as jnp
from jax import lax
from jax.experimental import pallas as pl
from jax.experimental.pallas import tpu as pltpu
from jax.sharding import PartitionSpec as P

MESH = pl.DeviceIdType.MESH
F32, BF16, I32 = jnp.float32, jnp.bfloat16, jnp.int32
N_X, N_Y, N_Z = 4, 4, 8
N_DP, N_SEQ = 16, 16
COARSE, FINE, C_IN, C_OUT, EMB = 256, 512, 1024, 768, 768
EXT = COARSE + 16
TAPS, ACAP, SLOTS = 5, 8, 64
CAP = N_SEQ * ACAP
TILE = 256
HALF = 384
BLOCK = 256
ROWS_SEQ = C_OUT // N_SEQ
INV_ROOT = 1.0 / math.sqrt(EMB)
K0 = math.sqrt(2.0 / math.pi)
K1 = 0.044715


def dot(a, b):
    return jnp.dot(a, b, preferred_element_type=F32)


def dot_nt(a, b):
    return lax.dot_general(a, b, (((1,), (1,)), ((), ())), preferred_element_type=F32)


def dot_tn(a, b):
    return lax.dot_general(a, b, (((0,), (0,)), ((), ())), preferred_element_type=F32)


def one_hot(condition):
    return jnp.where(condition, 1.0, 0.0).astype(BF16)


def iota(shape, axis):
    return lax.broadcasted_iota(I32, shape, axis)


def as_column(row):
    return jnp.transpose(jnp.broadcast_to(row, (128, 128)))[:, 0:1]


def as_row(column):
    return jnp.transpose(jnp.broadcast_to(column, (128, 128)))[0:1, :]


def folded(row):
    return jnp.where(row < 0, -1, (row & 1) * COARSE + (row >> 1))


def pack(rows):
    cells = rows.reshape(N_SEQ, ACAP, EMB)
    return jnp.concatenate([cells[:, :, :HALF], cells[:, :, HALF:]], axis=1).astype(BF16)


def unpack(cells):
    wide = cells.astype(F32)
    both = jnp.concatenate([wide[:, :ACAP], wide[:, ACAP:]], axis=2)
    return both.reshape(CAP, EMB).astype(BF16)


def kernel(
    coarse, skip, conv_w, donor_w, acceptor_w, other, score_grad, donor_pos, acceptor_pos, mask,
    scores_out, coarse_out, donor_out, acceptor_out,
    w, wd, wa, c_ext, skip_in, other_in, skip_f, other_f, act, slope,
    halo_next, halo_prev, grad_next, grad_prev, grad_left, grad_right,
    pos_own, pos_all, a1_send, a1_recv, a2_send, a2_recv,
    pe, po, out_v, dact, dgrad, aact, agrad,
    f_act, f_grad, sum1, part2, sum2, part3, piece, pieces,
    load_sem, w_sem, out_sem, halo_ssem, halo_rsem, ghalo_ssem, ghalo_rsem,
    pos_ssem, pos_rsem, a1_ssem, a1_rsem, a2_ssem, a2_rsem,
    f_ssem, f_rsem, g_ssem, g_rsem, local_sem,
    s2_ssem, s2_rsem, s3_ssem, s3_rsem, ag_ssem, ag_rsem,
):
    dp, seq = lax.axis_index("dp"), lax.axis_index("seq")
    x, yh, core = dp // 4, (dp // 2) % 2, dp % 2
    z, yl = seq // 2, seq % 2
    y = yh * 2 + yl

    loads = [
        pltpu.make_async_copy(coarse.at[0], c_ext.at[pl.ds(0, COARSE)], load_sem.at[0]),
        pltpu.make_async_copy(skip.at[0], skip_in, load_sem.at[1]),
        pltpu.make_async_copy(donor_w, wd, load_sem.at[2]),
        pltpu.make_async_copy(acceptor_w, wa, load_sem.at[3]),
        pltpu.make_async_copy(other.at[0], other_in, load_sem.at[4]),
    ]

    def load_w(n):
        cols = pl.ds(pl.multiple_of(n * TILE, TILE), TILE)
        return pltpu.make_async_copy(conv_w.at[:, :, cols], w.at[:, :, cols], w_sem.at[n])

    loads[0].start()
    loads[1].start()
    for n in range(C_OUT // TILE):
        load_w(n).start()
    loads[2].start()
    loads[3].start()
    loads[4].start()

    halo_next[...] = jnp.zeros_like(halo_next)
    halo_prev[...] = jnp.zeros_like(halo_prev)
    grad_next[...] = jnp.zeros_like(grad_next)
    grad_prev[...] = jnp.zeros_like(grad_prev)
    own_row = jnp.concatenate([acceptor_pos[...], jnp.full((1, 64), -1, I32)], axis=1)
    pos_own[...] = jnp.broadcast_to(own_row, (8, 128))

    barrier = pltpu.get_barrier_semaphore()

    def greet_seq(i, carry):
        pl.semaphore_signal(barrier, inc=1, device_id=(dp, (seq + i) % N_SEQ), device_id_type=MESH)
        return carry

    def greet_dp(i, carry):
        other_dp = (dp + i) % N_DP
        pl.semaphore_signal(barrier, inc=1, device_id=(other_dp, seq), device_id_type=MESH)
        pl.semaphore_signal(
            barrier, inc=1, device_id=(other_dp, z * 2 + 1 - yl), device_id_type=MESH
        )
        return carry

    lax.fori_loop(1, N_SEQ, greet_seq, 0)
    lax.fori_loop(1, N_DP, greet_dp, 0)
    pl.semaphore_wait(barrier, N_SEQ - 1 + 2 * (N_DP - 1))

    loads[0].wait()

    def halo_left():
        return pltpu.make_async_remote_copy(
            c_ext.at[pl.ds(0, 16)], halo_next, halo_ssem.at[0], halo_rsem.at[0],
            device_id=(dp, (seq + N_SEQ - 1) % N_SEQ), device_id_type=MESH)

    def halo_right():
        return pltpu.make_async_remote_copy(
            c_ext.at[pl.ds(COARSE - 16, 16)], halo_prev, halo_ssem.at[1], halo_rsem.at[1],
            device_id=(dp, (seq + 1) % N_SEQ), device_id_type=MESH)

    @pl.when(seq > 0)
    def _():
        halo_left().start()

    @pl.when(seq < N_SEQ - 1)
    def _():
        halo_right().start()

    def pos_copy(i):
        return pltpu.make_async_remote_copy(
            pos_own, pos_all.at[seq], pos_ssem.at[i], pos_rsem.at[seq],
            device_id=(dp, (seq + i) % N_SEQ), device_id_type=MESH)

    def pos_start(i, carry):
        pos_copy(i).start()
        return carry

    lax.fori_loop(1, N_SEQ, pos_start, 0)
    pos_all[seq] = pos_own[...]

    loads[1].wait()
    at = iota((COARSE, FINE), 1)
    step2 = 2 * iota((COARSE, FINE), 0)
    even, odd = one_hot(at == step2), one_hot(at == step2 + 1)
    skip_f[pl.ds(0, COARSE)] = dot(even, skip_in[...]).astype(BF16)
    skip_f[pl.ds(COARSE, COARSE)] = dot(odd, skip_in[...]).astype(BF16)

    sub, lane = iota((128, 128), 0), iota((128, 128), 1)
    before = one_hot(sub < lane)
    place = sub % ACAP
    own = jnp.broadcast_to(own_row, (128, 128))
    own_hit = (own >> 9) == sub // ACAP
    own_rank = dot(one_hot(own_hit), before).astype(I32)
    to_served = jnp.where(own_hit & (own_rank == place), 1.0, 0.0)
    from_served = jnp.transpose(to_served)[:SLOTS].astype(BF16)
    to_served = to_served[:, :SLOTS].astype(BF16)
    pad = jnp.full((1, 64), -1, I32)
    donor_row = folded(jnp.concatenate([donor_pos[...], pad], axis=1))
    donor_column = as_column(donor_row.astype(F32)).astype(I32)[:SLOTS]
    from_donor = one_hot(iota((SLOTS, FINE), 1) == donor_column)
    to_donor = one_hot(iota((FINE, 128), 0) == donor_row)
    fpad = jnp.zeros((1, 64), F32)
    mask_column = as_column(jnp.concatenate([mask[...].astype(F32), fpad], axis=1))[:SLOTS]
    score_column = as_column(jnp.concatenate([score_grad[...], fpad], axis=1))[:SLOTS]
    weighted = score_column * mask_column

    @pl.when(seq < N_SEQ - 1)
    def _():
        halo_left().wait_recv()

    @pl.when(seq > 0)
    def _():
        halo_right().wait_recv()

    row16 = iota((16, C_IN), 0)
    c_ext[pl.ds(COARSE, 16)] = jnp.where(
        row16 == 0, halo_next[...].astype(F32),
        jnp.where(row16 == 15, halo_prev[...].astype(F32), 0.0),
    ).astype(BF16)

    def conv_tile(n, carry):
        load_w(n).wait()
        cols = pl.ds(pl.multiple_of(n * TILE, TILE), TILE)
        cells = c_ext[...]
        taps = [dot(cells, w[k, :, cols]) for k in range(TAPS)]
        even_sum = (
            pltpu.roll(taps[0] + taps[1], 1, 0) + taps[2] + taps[3] + pltpu.roll(taps[4], EXT - 1, 0)
        )
        odd_sum = (
            pltpu.roll(taps[0], 1, 0) + taps[1] + taps[2] + pltpu.roll(taps[3] + taps[4], EXT - 1, 0)
        )
        for part, total in ((0, even_sum), (1, odd_sum)):
            rows = pl.ds(part * COARSE, COARSE)
            v = total[:COARSE] + skip_f[rows, cols].astype(F32)
            square = v * v
            t = jnp.tanh(K0 * v * (1.0 + K1 * square))
            half = 0.5 * (1.0 + t)
            act[rows, cols] = (v * half).astype(BF16)
            slope[rows, cols] = half + 0.5 * v * (1.0 - t * t) * (K0 * (1.0 + 3.0 * K1 * square))
        return carry

    lax.fori_loop(0, C_OUT // TILE, conv_tile, 0)

    def pos_wait(i, carry):
        src = (seq + i) % N_SEQ
        pltpu.make_async_remote_copy(
            pos_own, pos_all.at[src], pos_ssem.at[i], pos_rsem.at[src],
            device_id=(dp, src), device_id_type=MESH).wait_recv()
        return carry

    lax.fori_loop(1, N_SEQ, pos_wait, 0)
    named = pos_all[...].reshape(CAP, 128)
    hit = (named >> 9) == seq
    rank = dot(one_hot(hit), before).astype(I32)
    chosen = jnp.where(hit & (rank == place), (named & (FINE - 1)) + 1, 0).astype(F32)
    served = jnp.sum(chosen, axis=1, keepdims=True).astype(I32) - 1
    served = folded(served)
    from_rows = one_hot(iota((CAP, FINE), 1) == served)
    served_row = as_row(served.astype(F32)).astype(I32)
    to_rows = one_hot(iota((FINE, CAP), 0) == served_row)
    a1_send[...] = pack(dot(from_rows, act[...]))

    def exchange(send, recv, ssem, rsem):
        def copy(i):
            peer = (seq + i) % N_SEQ
            return pltpu.make_async_remote_copy(
                send.at[peer], recv.at[seq], ssem.at[i], rsem.at[seq],
                device_id=(dp, peer), device_id_type=MESH)

        def start(i, carry):
            copy(i).start()
            return carry

        def wait(i, carry):
            src = (seq + i) % N_SEQ
            pltpu.make_async_remote_copy(
                send.at[src], recv.at[src], ssem.at[i], rsem.at[src],
                device_id=(dp, src), device_id_type=MESH).wait_recv()
            return carry

        def drain(i, carry):
            copy(i).wait_send()
            return carry

        return [lambda f=f: lax.fori_loop(1, N_SEQ, f, 0) for f in (start, wait, drain)]

    a1_start, a1_wait, a1_drain = exchange(a1_send, a1_recv, a1_ssem, a1_rsem)
    a2_start, a2_wait, a2_drain = exchange(a2_send, a2_recv, a2_ssem, a2_rsem)
    a1_start()
    a1_recv[seq] = a1_send[seq]

    loads[2].wait()
    loads[3].wait()
    donor_act = dot(from_donor, act[...]).astype(BF16)
    donor_emb = dot(donor_act, wd[...]).astype(BF16).astype(F32)
    acceptor_emb_grad = (weighted * donor_emb * INV_ROOT).astype(BF16)
    acceptor_rows = dot_nt(acceptor_emb_grad, wa[...]).astype(BF16)
    a2_send[...] = pack(dot(to_served, acceptor_rows))
    a2_start()
    a2_recv[seq] = a2_send[seq]
    dact[...] = donor_act
    agrad[...] = acceptor_emb_grad

    loads[4].wait()
    other_f[pl.ds(0, COARSE)] = dot(even, other_in[...]).astype(BF16)
    other_f[pl.ds(COARSE, COARSE)] = dot(odd, other_in[...]).astype(BF16)

    a1_wait()
    acceptor_act = dot(from_served, unpack(a1_recv[...])).astype(BF16)
    acceptor_emb = dot(acceptor_act, wa[...]).astype(BF16).astype(F32)
    score = mask_column * jnp.sum(donor_emb * acceptor_emb, axis=1, keepdims=True) * INV_ROOT
    score = jnp.concatenate([score, jnp.zeros((128 - SLOTS, 1), F32)], axis=0)
    scores_out[...] = as_row(score)[:, :SLOTS]
    donor_emb_grad = (weighted * acceptor_emb * INV_ROOT).astype(BF16)
    aact[...] = acceptor_act
    dgrad[...] = donor_emb_grad

    acts, grads = (dact, aact), (dgrad, agrad)

    def target(kind, p):
        if kind == 0:
            return (p * 4 + yh * 2, seq)
        return (x * 4 + (p // 2) * 2 + 1, z * 2 + p % 2)

    ring_at = (x, y)
    first = jnp.where(core == 0, x, y)
    second = jnp.where(core == 0, y, x)
    active = first < 3

    def factor_copies(kind, p, source):
        slot = kind * 3 + p
        cols = pl.ds(p * BLOCK, BLOCK)
        device = target(kind, p)
        return [
            pltpu.make_async_remote_copy(
                acts[kind], f_act.at[source], f_ssem.at[slot], f_rsem.at[source],
                device_id=device, device_id_type=MESH),
            pltpu.make_async_remote_copy(
                grads[kind].at[:, cols], f_grad.at[source], g_ssem.at[slot], g_rsem.at[source],
                device_id=device, device_id_type=MESH),
        ]

    for kind in range(2):
        source = ring_at[kind] * 2 + core
        for p in range(3):
            mine = (core == kind) & (ring_at[kind] == p)

            @pl.when(jnp.logical_not(mine))
            def _(kind=kind, p=p, source=source):
                for copy in factor_copies(kind, p, source):
                    copy.start()

            @pl.when(mine)
            def _(kind=kind, p=p, source=source):
                f_act[source] = acts[kind][...]
                f_grad[source] = grads[kind][:, p * BLOCK:(p + 1) * BLOCK]

    donor_rows = dot_nt(donor_emb_grad, wd[...]).astype(BF16)
    a2_wait()
    served_rows = unpack(a2_recv[...])

    def grad_of(rows):
        total = (
            other_f[rows].astype(F32)
            + dot(to_rows[rows.start:rows.start + rows.size], served_rows)
            + dot(to_donor[rows.start:rows.start + rows.size, :SLOTS], donor_rows)
        )
        return total * slope[rows]

    g_even = grad_of(pl.ds(0, COARSE))
    g_odd = grad_of(pl.ds(COARSE, COARSE))
    pair = g_even + g_odd
    pe[pl.ds(0, COARSE)] = pair.astype(BF16)
    grad_left[pl.ds(0, 16)] = pair[:16].astype(BF16)
    grad_left[pl.ds(16, 16)] = g_even[:16].astype(BF16)
    grad_right[pl.ds(0, 16)] = pair[COARSE - 16:].astype(BF16)
    grad_right[pl.ds(16, 16)] = g_odd[COARSE - 16:].astype(BF16)

    def ghalo_left():
        return pltpu.make_async_remote_copy(
            grad_left, grad_next, ghalo_ssem.at[0], ghalo_rsem.at[0],
            device_id=(dp, (seq + N_SEQ - 1) % N_SEQ), device_id_type=MESH)

    def ghalo_right():
        return pltpu.make_async_remote_copy(
            grad_right, grad_prev, ghalo_ssem.at[1], ghalo_rsem.at[1],
            device_id=(dp, (seq + 1) % N_SEQ), device_id_type=MESH)

    @pl.when(seq > 0)
    def _():
        ghalo_left().start()

    @pl.when(seq < N_SEQ - 1)
    def _():
        ghalo_right().start()

    shifted = pltpu.roll(g_odd, 1, 0)
    po[pl.ds(0, COARSE)] = (shifted + g_even).astype(BF16)

    @pl.when(seq < N_SEQ - 1)
    def _():
        ghalo_left().wait_recv()

    @pl.when(seq > 0)
    def _():
        ghalo_right().wait_recv()

    grow = iota((16, C_OUT), 0)
    after = grad_next[...].astype(F32)
    prior = grad_prev[...].astype(F32)
    pe[pl.ds(COARSE, 16)] = jnp.where(
        grow == 0, after[:16], jnp.where(grow == 15, prior[:16], 0.0)
    ).astype(BF16)
    prior_odd = pltpu.roll(prior[16:], 1, 0)
    po[pl.ds(0, 16)] = (
        jnp.where(grow == 0, prior_odd, shifted[:16]) + g_even[:16]
    ).astype(BF16)
    last_odd = pltpu.roll(g_odd[COARSE - 16:], 1, 0)
    po[pl.ds(COARSE, 16)] = jnp.where(grow == 0, last_odd + after[16:], 0.0).astype(BF16)

    def out_copy(n):
        cols = pl.ds(pl.multiple_of(n * TILE, TILE), TILE)
        return pltpu.make_async_copy(out_v.at[:, cols], coarse_out.at[0, :, cols], out_sem.at[n])

    def back_tile(n, carry):
        cols = pl.ds(pl.multiple_of(n * TILE, TILE), TILE)
        pairs, cross = pe[...], po[...]
        ahead = dot_nt(pairs, w[0, cols, :]) + dot_nt(cross, w[1, cols, :])
        here = dot_nt(pairs[:COARSE], w[2, cols, :]) + dot_nt(cross[:COARSE], w[3, cols, :])
        behind = dot_nt(pairs, w[4, cols, :])
        total = here + pltpu.roll(ahead, EXT - 1, 0)[:COARSE] + pltpu.roll(behind, 1, 0)[:COARSE]
        out_v[:, cols] = total.astype(BF16)
        out_copy(n).start()
        return carry

    lax.fori_loop(0, C_IN // TILE, back_tile, 0)

    sources = 8

    def second_device(r):
        if_donor = x * 4 + (r // 2) * 2
        if_acceptor = r * 4 + yh * 2 + 1
        return (
            jnp.where(core == 0, if_donor, if_acceptor),
            jnp.where(core == 0, z * 2 + r % 2, seq),
        )

    def chunk_copy(r, source):
        return pltpu.make_async_remote_copy(
            sum1.at[:, r % 2, :, pl.ds((r // 2) * 128, 128)], part2.at[source],
            s2_ssem.at[r], s2_rsem.at[source], device_id=second_device(r), device_id_type=MESH)

    def z_device(zt):
        return (dp, zt * 2 + yl)

    def z_copy(i):
        zt = (z + i) % N_Z
        return pltpu.make_async_remote_copy(
            sum2.at[zt], part3.at[z], s3_ssem.at[i], s3_rsem.at[z],
            device_id=z_device(zt), device_id_type=MESH)

    tile_at = first * 2 + second // 2
    seq_to = z * 2 + second % 2

    def gather_copy(d):
        return pltpu.make_async_remote_copy(
            piece, pieces.at[core, tile_at], ag_ssem.at[d], ag_rsem.at[core, tile_at],
            device_id=(d, seq_to), device_id_type=MESH)

    @pl.when(active)
    def _():
        for s in range(sources):
            @pl.when(s != first * 2 + core)
            def _(s=s):
                for kind in range(2):
                    @pl.when(core == kind)
                    def _(kind=kind):
                        for copy in factor_copies(kind, 0, s):
                            copy.wait_recv()

        for m in range(C_OUT // TILE):
            left = f_act[:, :, m * TILE:(m + 1) * TILE].reshape(sources * SLOTS, TILE)
            right = f_grad[...].reshape(sources * SLOTS, BLOCK)
            block = dot_tn(left, right).astype(BF16)
            for g in range(TILE // 16):
                row = m * TILE + g * 16
                s, at_row = row // ROWS_SEQ, row % ROWS_SEQ
                sum1[s // 2, s % 2, at_row:at_row + 16, :] = block[g * 16:(g + 1) * 16]
        for r in range(4):
            @pl.when(r != second)
            def _(r=r):
                chunk_copy(r, second).start()

            @pl.when(r == second)
            def _(r=r):
                part2[r] = sum1[:, r % 2, :, (r // 2) * 128:(r // 2) * 128 + 128]

        for r in range(4):
            @pl.when(r != second)
            def _(r=r):
                chunk_copy(r, r).wait_recv()

        sum2[...] = (
            part2[0].astype(F32) + part2[1].astype(F32) + part2[2].astype(F32) + part2[3].astype(F32)
        ).astype(BF16)

        for i in range(1, N_Z):
            z_copy(i).start()
        part3[z] = sum2[z]
        for i in range(1, N_Z):
            src = (z + i) % N_Z
            pltpu.make_async_remote_copy(
                sum2.at[src], part3.at[src], s3_ssem.at[i], s3_rsem.at[src],
                device_id=z_device(src), device_id_type=MESH).wait_recv()
        total = part3[0].astype(F32)
        for i in range(1, N_Z):
            total = total + part3[i].astype(F32)
        piece[...] = (total * (1.0 / N_DP)).astype(BF16)

        for d in range(N_DP):
            mine = (d == dp) & (seq_to == seq)

            @pl.when(jnp.logical_not(mine))
            def _(d=d):
                gather_copy(d).start()

            @pl.when(mine)
            def _(d=d):
                pieces[core, tile_at] = piece[...]

    for kind, out in ((0, donor_out), (1, acceptor_out)):
        for t in range(6):
            if kind == 0:
                source = ((t // 2) * 4 + (t % 2) * 2, seq)
            else:
                y_s = t // 2
                source = (((t % 2) * 2 + yl) * 4 + (y_s // 2) * 2 + 1, z * 2 + y_s % 2)
            mine = (source[0] == dp) & (source[1] == seq)

            @pl.when(jnp.logical_not(mine))
            def _(kind=kind, t=t, source=source):
                pltpu.make_async_remote_copy(
                    piece, pieces.at[kind, t], ag_ssem.at[0], ag_rsem.at[kind, t],
                    device_id=source, device_id_type=MESH).wait_recv()

            out[:, t * 128:(t + 1) * 128] = pieces[kind, t].astype(F32)

    lax.fori_loop(0, C_IN // TILE, lambda n, carry: (out_copy(n).wait(), carry)[1], 0)

    @pl.when(seq > 0)
    def _():
        halo_left().wait_send()
        ghalo_left().wait_send()

    @pl.when(seq < N_SEQ - 1)
    def _():
        halo_right().wait_send()
        ghalo_right().wait_send()

    lax.fori_loop(1, N_SEQ, lambda i, carry: (pos_copy(i).wait_send(), carry)[1], 0)
    a1_drain()
    a2_drain()
    for kind in range(2):
        for p in range(3):
            mine = (core == kind) & (ring_at[kind] == p)

            @pl.when(jnp.logical_not(mine))
            def _(kind=kind, p=p):
                for copy in factor_copies(kind, p, 0):
                    copy.wait_send()

    @pl.when(active)
    def _():
        for r in range(4):
            @pl.when(r != second)
            def _(r=r):
                chunk_copy(r, second).wait_send()
        for i in range(1, N_Z):
            z_copy(i).wait_send()
        for d in range(N_DP):
            @pl.when(jnp.logical_not((d == dp) & (seq_to == seq)))
            def _(d=d):
                gather_copy(d).wait_send()


def on_device(*args):
    vmem = pl.BlockSpec(memory_space=pltpu.VMEM)
    hbm = pl.BlockSpec(memory_space=pl.ANY)
    dma = pltpu.SemaphoreType.DMA

    def v(*shape, dtype=BF16):
        return pltpu.VMEM(shape, dtype)

    scratch = [
        v(TAPS, C_IN, C_OUT), v(C_OUT, EMB), v(C_OUT, EMB), v(EXT, C_IN),
        v(FINE, C_OUT), v(FINE, C_OUT), v(FINE, C_OUT), v(FINE, C_OUT),
        v(FINE, C_OUT), v(FINE, C_OUT, dtype=F32),
        v(16, C_IN), v(16, C_IN), v(32, C_OUT), v(32, C_OUT), v(32, C_OUT), v(32, C_OUT),
        v(8, 128, dtype=I32), v(N_SEQ, 8, 128, dtype=I32),
        v(N_SEQ, 16, HALF), v(N_SEQ, 16, HALF), v(N_SEQ, 16, HALF), v(N_SEQ, 16, HALF),
        v(EXT, C_OUT), v(EXT, C_OUT), v(COARSE, C_IN),
        v(SLOTS, C_OUT), v(SLOTS, EMB), v(SLOTS, C_OUT), v(SLOTS, EMB),
        v(8, SLOTS, C_OUT), v(8, SLOTS, BLOCK), v(N_Z, 2, ROWS_SEQ, BLOCK),
        v(4, N_Z, ROWS_SEQ, 128), v(N_Z, ROWS_SEQ, 128), v(N_Z, ROWS_SEQ, 128),
        v(ROWS_SEQ, 128), v(2, 6, ROWS_SEQ, 128),
        dma((5,)), dma((3,)), dma((4,)), dma((2,)), dma((2,)), dma((2,)), dma((2,)),
        dma((N_SEQ,)), dma((N_SEQ,)), dma((N_SEQ,)), dma((N_SEQ,)), dma((N_SEQ,)), dma((N_SEQ,)),
        dma((6,)), dma((8,)), dma((6,)), dma((8,)), dma((2,)),
        dma((4,)), dma((4,)), dma((N_Z,)), dma((N_Z,)), dma((N_DP,)), dma((2, 6)),
    ]
    return pl.pallas_call(
        kernel,
        out_shape=(
            jax.ShapeDtypeStruct((1, SLOTS), F32),
            jax.ShapeDtypeStruct((1, COARSE, C_IN), BF16),
            jax.ShapeDtypeStruct((ROWS_SEQ, EMB), F32),
            jax.ShapeDtypeStruct((ROWS_SEQ, EMB), F32),
        ),
        in_specs=[hbm] * 6 + [vmem] * 4,
        out_specs=(vmem, hbm, vmem, vmem),
        scratch_shapes=scratch,
        compiler_params=pltpu.CompilerParams(
            collective_id=0, has_side_effects=True, vmem_limit_bytes=48 * 1024 * 1024
        ),
    )(*args)


def solution(mesh):
    rows, slots = P("dp", "seq", None), P("dp", "seq")
    return jax.shard_map(
        on_device,
        mesh=mesh,
        in_specs=(rows, rows, P(), P(), P(), rows, slots, slots, slots, slots),
        out_specs=(slots, rows, P("seq", None), P("seq", None)),
        check_vma=False,
    )
```

time: 380 us -> 68.3 us (0.18)
  waiting for transfers between devices: 258 us -> 0 us
  Pallas kernels: 0 us -> 56.3 us
  matrix products: 39.9 us -> 0 us
  starting transfers between devices: 31.8 us -> 0 us
  other arithmetic: 18.9 us -> 0 us
  between operations: 14.5 us -> 0.66 us
  local copies, waits for them, and re-layouts: 15.4 us -> 11.1 us
    psum x1 -> x0, waiting for transfers between devices: 247 us -> none  [on_device(): lax.psum((donor_term, acceptor_term), ('dp', 'seq'))]
    pallas_call x0 -> x1, Pallas kernels: none -> 56.3 us  [on_device(): pl.pallas_call(kernel, out_shape=(jax.ShapeDtypeStruct((1, SLOTS), F32),...]
    dot_general x16 -> x0, matrix products: 39.9 us -> none  [the longest x5 20.8 us: on_device(): jnp.dot(upsampled[shift_index:shift_index + row_count], conv_weight[shift...]
    all_to_all x3 -> x0, starting transfers between devices: 20.7 us -> none  [the longest x1 11.2 us: on_device(): lax.all_to_all(requests, 'seq', split_axis=0, concat_axis=0, tiled=True)]
    all_to_all x3 -> x0, waiting for transfers between devices: 11.6 us -> none  [the longest x1 6.48 us: on_device(): lax.all_to_all(projected, 'seq', split_axis=0, concat_axis=0, tiled=True)]
    unnamed x26 -> x22, local copies, waits for them, and re-layouts: 0.09 us -> 11.1 us
    ppermute x4 -> x0, starting transfers between devices: 10.9 us -> none  [the longest x2 8.01 us: with_halo(): lax.ppermute(tail, axis, [(i, (i + 1) % count) for i in range(ends)])]
    scatter-add x2 -> x0, other arithmetic: 4.04 us -> none  [the longest x1 2.45 us: on_device(): act_grad.at[served_flat].add(row_terms.reshape(-1, row_terms.shape[2]))]
  transfers between devices with their start and end apart: 8 -> 0, of which waited for: 4 -> 0; matrix products, arithmetic and copies ran while one was open for 9% -> 0% of each run, Pallas kernels for 0% -> 0%
where the time goes in v1:
time: 68.3 us; the launch traced here: 68 us
  Pallas kernels  56.3 us (82%)
  local copies, waits for them, and re-layouts  11.1 us (16%)
    pallas_call x1, Pallas kernels, on_device(): pl.pallas_call(kernel, out_shape=(jax.ShapeDtypeStruct((1, SLOTS), F32),...  56.3 us
    unnamed x22, local copies, waits for them, and re-layouts  11.1 us

profile of v1, /device:TPU:1, one launch (start us, length us, event | category | flops | bytes accessed | tf_op | source)
XLA Modules:
  0.0 68.0 jit_solution(12105005993104042299)
XLA Ops:
  0.6 0.0 copy-start
  0.6 1.3 %copy-done = bf16[768,768]{1,0:T(8,128)(2,1)S(1)} copy-done((bf16[768,768]{1,0:T(8,128)(2,1)S(1)}, bf16[768,768]{1,0:T(8,128)(2,1)}, u32[]{:S(2)}) %copy-start) | copy-done | bytes 1179672
  1.9 0.0 copy-start.1
  1.9 1.3 %copy-done.1 = bf16[768,768]{1,0:T(8,128)(2,1)S(1)} copy-done((bf16[768,768]{1,0:T(8,128)(2,1)S(1)}, bf16[768,768]{1,0:T(8,128)(2,1)}, u32[]{:S(2)}) %copy-start.1) | copy-done | bytes 1179672
  3.2 0.0 copy-start.2
  3.2 1.1 %copy-done.2 = bf16[1,512,768]{2,1,0:T(8,128)(2,1)S(1)} copy-done((bf16[1,512,768]{2,1,0:T(8,128)(2,1)S(1)}, bf16[1,512,768]{2,1,0:T(8,128)(2,1)}, u32[]{:S(2)}) %copy-start.2) | copy-done | bytes 786456
  4.3 0.0 copy-start.3
  4.3 1.1 %copy-done.3 = bf16[1,512,768]{2,1,0:T(8,128)(2,1)S(1)} copy-done((bf16[1,512,768]{2,1,0:T(8,128)(2,1)S(1)}, bf16[1,512,768]{2,1,0:T(8,128)(2,1)}, u32[]{:S(2)}) %copy-start.3) | copy-done | bytes 786456
  5.4 0.0 copy-start.4
  5.4 1.0 %copy-done.4 = bf16[1,256,1024]{2,1,0:T(8,128)(2,1)S(1)} copy-done((bf16[1,256,1024]{2,1,0:T(8,128)(2,1)S(1)}, bf16[1,256,1024]{2,1,0:T(8,128)(2,1)}, u32[]{:S(2)}) %copy-start.4) | copy-done | bytes 524312
  6.5 0.0 copy-start.5
  6.5 0.7 copy-done.5
  7.1 0.0 copy-start.6
  7.1 0.7 copy-done.6
  7.8 0.0 copy-start.7
  7.8 0.7 copy-done.7
  8.5 0.0 copy-start.8
  8.5 0.7 copy-done.8
  9.1 56.3 %shard_map.129 = (f32[1,64]{1,0:T(1,128)S(1)}, bf16[1,256,1024]{2,1,0:T(8,128)(2,1)S(1)}, f32[48,768]{1,0:T(8,128)S(1)}, f32[48,768]{1,0:T(8,128)S(1)}) custom-call(bf16[1,256,1024]{2,1,0:T(8,128)(2,1)S(1)} %copy-done.4, bf16[1,512,768]{2,1,0:T(8,128)(2,1)S(1)} %copy-done.2, bf16[5,1024,768]{2,1,0:T(8,128)(2,1)} %conv_w.1, bf16[768,768]{1,0:T(8,128)(2,1)S(1)} %copy-done, ...), custom_call_target="tpu_custom_call" | custom-call | tf_op jit(solution)/shard_map/pallas_call | solution.py:595
  65.4 0.5 copy.18
  65.9 0.8 %copy.19 = bf16[1,256,1024]{2,1,0:T(8,128)(2,1)} copy(bf16[1,256,1024]{2,1,0:T(8,128)(2,1)S(1)} %get-tuple-element.9) | data formatting | bytes 1048576
  66.7 0.7 copy.20
  67.4 0.7 copy.21
Async XLA Ops:
  0.6 1.3 %copy-start = (bf16[768,768]{1,0:T(8,128)(2,1)S(1)}, bf16[768,768]{1,0:T(8,128)(2,1)}, u32[]{:S(2)}) copy-start(bf16[768,768]{1,0:T(8,128)(2,1)} %donor_w.1) | copy-start | bytes 3538948
  1.9 1.3 %copy-start.1 = (bf16[768,768]{1,0:T(8,128)(2,1)S(1)}, bf16[768,768]{1,0:T(8,128)(2,1)}, u32[]{:S(2)}) copy-start(bf16[768,768]{1,0:T(8,128)(2,1)} %acceptor_w.1) | copy-start | bytes 3538948
  3.2 1.1 %copy-start.2 = (bf16[1,512,768]{2,1,0:T(8,128)(2,1)S(1)}, bf16[1,512,768]{2,1,0:T(8,128)(2,1)}, u32[]{:S(2)}) copy-start(bf16[1,512,768]{2,1,0:T(8,128)(2,1)} %skip.1) | copy-start | bytes 2359300
  4.3 1.1 %copy-start.3 = (bf16[1,512,768]{2,1,0:T(8,128)(2,1)S(1)}, bf16[1,512,768]{2,1,0:T(8,128)(2,1)}, u32[]{:S(2)}) copy-start(bf16[1,512,768]{2,1,0:T(8,128)(2,1)} %other.1) | copy-start | bytes 2359300
  5.4 1.0 %copy-start.4 = (bf16[1,256,1024]{2,1,0:T(8,128)(2,1)S(1)}, bf16[1,256,1024]{2,1,0:T(8,128)(2,1)}, u32[]{:S(2)}) copy-start(bf16[1,256,1024]{2,1,0:T(8,128)(2,1)} %coarse.1) | copy-start | bytes 1572868
  6.5 0.7 copy-start.5
  7.1 0.7 copy-start.6
  7.8 0.7 copy-start.7
  8.5 0.7 copy-start.8

commit v2 on v1

v2 whole, which is shorter than its diff:
```python
import math

import jax
import jax.numpy as jnp
from jax import lax
from jax.experimental import pallas as pl
from jax.experimental.pallas import tpu as pltpu
from jax.sharding import PartitionSpec as P

MESH = pl.DeviceIdType.MESH
F32, BF16, I32 = jnp.float32, jnp.bfloat16, jnp.int32
N_X, N_Y, N_Z = 4, 4, 8
N_DP, N_SEQ = 16, 16
COARSE, FINE, C_IN, C_OUT, EMB = 256, 512, 1024, 768, 768
EXT = COARSE + 16
TAPS, ACAP, SLOTS = 5, 8, 64
CAP = N_SEQ * ACAP
TILE = 256
HALF = 384
BLOCK = 256
ROWS_SEQ = C_OUT // N_SEQ
INV_ROOT = 1.0 / math.sqrt(EMB)
K0 = math.sqrt(2.0 / math.pi)
K1 = 0.044715


def dot(a, b):
    return jnp.dot(a, b, preferred_element_type=F32)


def dot_nt(a, b):
    return lax.dot_general(a, b, (((1,), (1,)), ((), ())), preferred_element_type=F32)


def dot_tn(a, b):
    return lax.dot_general(a, b, (((0,), (0,)), ((), ())), preferred_element_type=F32)


def one_hot(condition):
    return jnp.where(condition, 1.0, 0.0).astype(BF16)


def iota(shape, axis):
    return lax.broadcasted_iota(I32, shape, axis)


def as_column(row):
    return jnp.transpose(jnp.broadcast_to(row, (128, 128)))[:, 0:1]


def as_row(column):
    return jnp.transpose(jnp.broadcast_to(column, (128, 128)))[0:1, :]


def folded(row):
    return jnp.where(row < 0, -1, (row & 1) * COARSE + (row >> 1))


def pack(rows):
    cells = rows.reshape(N_SEQ, ACAP, EMB)
    return jnp.concatenate([cells[:, :, :HALF], cells[:, :, HALF:]], axis=1).astype(BF16)


def unpack(cells):
    wide = cells.astype(F32)
    both = jnp.concatenate([wide[:, :ACAP], wide[:, ACAP:]], axis=2)
    return both.reshape(CAP, EMB).astype(BF16)


def kernel(
    coarse, skip, conv_w, donor_w, acceptor_w, other, score_grad, donor_pos, acceptor_pos, mask,
    scores_out, coarse_out, donor_out, acceptor_out,
    score_v, donor_v, acceptor_v, mask_v, w, wd, wa, c_ext, skip_in, other_in, skip_f, other_f, act, slope,
    halo_next, halo_prev, grad_next, grad_prev, grad_left, grad_right,
    pos_own, pos_all, a1_send, a1_recv, a2_send, a2_recv,
    pe, po, dact, dgrad, aact, agrad,
    f_act, f_grad, sum1, part2, sum2, part3, piece, pieces,
    load_sem, w_sem, halo_ssem, halo_rsem, ghalo_ssem, ghalo_rsem,
    pos_ssem, pos_rsem, a1_ssem, a1_rsem, a2_ssem, a2_rsem,
    f_ssem, f_rsem, g_ssem, g_rsem,
    s2_ssem, s2_rsem, s3_ssem, s3_rsem, ag_ssem, ag_rsem,
):
    dp, seq = lax.axis_index("dp"), lax.axis_index("seq")
    x, yh, core = dp // 4, (dp // 2) % 2, dp % 2
    z, yl = seq // 2, seq % 2
    y = yh * 2 + yl

    drains = []

    def finish():
        for drain in drains:
            drain()

    def when(condition, action):
        pl.when(condition)(action)

    smalls = (score_grad, donor_pos, acceptor_pos, mask)
    held = (score_v, donor_v, acceptor_v, mask_v)
    small_loads = [
        pltpu.make_async_copy(a, b, load_sem.at[5 + i]) for i, (a, b) in enumerate(zip(smalls, held))
    ]
    loads = [
        pltpu.make_async_copy(coarse.at[0], c_ext.at[pl.ds(0, COARSE)], load_sem.at[0]),
        pltpu.make_async_copy(skip.at[0], skip_in, load_sem.at[1]),
        pltpu.make_async_copy(donor_w, wd, load_sem.at[2]),
        pltpu.make_async_copy(acceptor_w, wa, load_sem.at[3]),
        pltpu.make_async_copy(other.at[0], other_in, load_sem.at[4]),
    ]

    def load_w(n):
        cols = pl.ds(pl.multiple_of(n * TILE, TILE), TILE)
        return pltpu.make_async_copy(conv_w.at[:, :, cols], w.at[:, :, cols], w_sem.at[n])

    for load in small_loads:
        load.start()
    loads[0].start()

    halo_next[...] = jnp.zeros_like(halo_next)
    halo_prev[...] = jnp.zeros_like(halo_prev)
    grad_next[...] = jnp.zeros_like(grad_next)
    grad_prev[...] = jnp.zeros_like(grad_prev)
    barrier = pltpu.get_barrier_semaphore()

    def greet_seq(i, carry):
        pl.semaphore_signal(barrier, inc=1, device_id=(dp, (seq + i) % N_SEQ), device_id_type=MESH)
        return carry

    def greet_dp(i, carry):
        other_dp = (dp + i) % N_DP
        pl.semaphore_signal(barrier, inc=1, device_id=(other_dp, seq), device_id_type=MESH)
        pl.semaphore_signal(
            barrier, inc=1, device_id=(other_dp, z * 2 + 1 - yl), device_id_type=MESH
        )
        return carry

    lax.fori_loop(1, N_SEQ, greet_seq, 0)
    lax.fori_loop(1, N_DP, greet_dp, 0)
    load_w(0).start()
    loads[1].start()
    for n in range(1, C_OUT // TILE):
        load_w(n).start()
    for load in loads[2:]:
        load.start()
    for load in small_loads:
        load.wait()
    own_row = jnp.concatenate([acceptor_v[...], jnp.full((1, 64), -1, I32)], axis=1)
    pos_own[...] = jnp.broadcast_to(own_row, (8, 128))
    loads[0].wait()
    pl.semaphore_wait(barrier, N_SEQ - 1 + 2 * (N_DP - 1))


    def halo_left():
        return pltpu.make_async_remote_copy(
            c_ext.at[pl.ds(0, 16)], halo_next, halo_ssem.at[0], halo_rsem.at[0],
            device_id=(dp, (seq + N_SEQ - 1) % N_SEQ), device_id_type=MESH)

    def halo_right():
        return pltpu.make_async_remote_copy(
            c_ext.at[pl.ds(COARSE - 16, 16)], halo_prev, halo_ssem.at[1], halo_rsem.at[1],
            device_id=(dp, (seq + 1) % N_SEQ), device_id_type=MESH)

    when(seq > 0, lambda: halo_left().start())
    when(seq < N_SEQ - 1, lambda: halo_right().start())
    drains.append(lambda: when(seq > 0, lambda: halo_left().wait_send()))
    drains.append(lambda: when(seq < N_SEQ - 1, lambda: halo_right().wait_send()))

    def pos_copy(i):
        return pltpu.make_async_remote_copy(
            pos_own, pos_all.at[seq], pos_ssem.at[i], pos_rsem.at[seq],
            device_id=(dp, (seq + i) % N_SEQ), device_id_type=MESH)

    def pos_start(i, carry):
        pos_copy(i).start()
        return carry

    lax.fori_loop(1, N_SEQ, pos_start, 0)
    drains.append(
        lambda: lax.fori_loop(1, N_SEQ, lambda i, carry: (pos_copy(i).wait_send(), carry)[1], 0)
    )
    pos_all[seq] = pos_own[...]

    loads[1].wait()
    at = iota((COARSE, FINE), 1)
    step2 = 2 * iota((COARSE, FINE), 0)
    even, odd = one_hot(at == step2), one_hot(at == step2 + 1)
    skip_f[pl.ds(0, COARSE)] = dot(even, skip_in[...]).astype(BF16)
    skip_f[pl.ds(COARSE, COARSE)] = dot(odd, skip_in[...]).astype(BF16)

    sub, lane = iota((128, 128), 0), iota((128, 128), 1)
    before = one_hot(sub < lane)
    place = sub % ACAP
    own = jnp.broadcast_to(own_row, (128, 128))
    own_hit = (own >> 9) == sub // ACAP
    own_rank = dot(one_hot(own_hit), before).astype(I32)
    to_served = jnp.where(own_hit & (own_rank == place), 1.0, 0.0)
    from_served = jnp.transpose(to_served)[:SLOTS].astype(BF16)
    to_served = to_served[:, :SLOTS].astype(BF16)
    pad = jnp.full((1, 64), -1, I32)
    donor_row = folded(jnp.concatenate([donor_v[...], pad], axis=1))
    donor_column = as_column(donor_row.astype(F32)).astype(I32)[:SLOTS]
    from_donor = one_hot(iota((SLOTS, FINE), 1) == donor_column)
    to_donor = one_hot(iota((FINE, 128), 0) == donor_row)
    fpad = jnp.zeros((1, 64), F32)
    mask_column = as_column(jnp.concatenate([mask_v[...].astype(F32), fpad], axis=1))[:SLOTS]
    score_column = as_column(jnp.concatenate([score_v[...], fpad], axis=1))[:SLOTS]
    weighted = score_column * mask_column

    when(seq < N_SEQ - 1, lambda: halo_left().wait_recv())
    when(seq > 0, lambda: halo_right().wait_recv())

    row16 = iota((16, C_IN), 0)
    c_ext[pl.ds(COARSE, 16)] = jnp.where(
        row16 == 0, halo_next[...].astype(F32),
        jnp.where(row16 == 15, halo_prev[...].astype(F32), 0.0),
    ).astype(BF16)

    def conv_tile(n, carry):
        load_w(n).wait()
        cols = pl.ds(pl.multiple_of(n * TILE, TILE), TILE)
        cells = c_ext[...]
        taps = [dot(cells, w[k, :, cols]) for k in range(TAPS)]
        even_sum = (
            pltpu.roll(taps[0] + taps[1], 1, 0) + taps[2] + taps[3] + pltpu.roll(taps[4], EXT - 1, 0)
        )
        odd_sum = (
            pltpu.roll(taps[0], 1, 0) + taps[1] + taps[2] + pltpu.roll(taps[3] + taps[4], EXT - 1, 0)
        )
        for part, total in ((0, even_sum), (1, odd_sum)):
            rows = pl.ds(part * COARSE, COARSE)
            v = total[:COARSE] + skip_f[rows, cols].astype(F32)
            square = v * v
            t = jnp.tanh(K0 * v * (1.0 + K1 * square))
            half = 0.5 * (1.0 + t)
            act[rows, cols] = (v * half).astype(BF16)
            slope[rows, cols] = half + 0.5 * v * (1.0 - t * t) * (K0 * (1.0 + 3.0 * K1 * square))
        return carry

    lax.fori_loop(0, C_OUT // TILE, conv_tile, 0)

    def pos_wait(i, carry):
        src = (seq + i) % N_SEQ
        pltpu.make_async_remote_copy(
            pos_own, pos_all.at[src], pos_ssem.at[i], pos_rsem.at[src],
            device_id=(dp, src), device_id_type=MESH).wait_recv()
        return carry

    lax.fori_loop(1, N_SEQ, pos_wait, 0)
    named = pos_all[...].reshape(CAP, 128)
    hit = (named >> 9) == seq
    rank = dot(one_hot(hit), before).astype(I32)
    chosen = jnp.where(hit & (rank == place), (named & (FINE - 1)) + 1, 0).astype(F32)
    served = jnp.sum(chosen, axis=1, keepdims=True).astype(I32) - 1
    served = folded(served)
    from_rows = one_hot(iota((CAP, FINE), 1) == served)
    served_row = as_row(served.astype(F32)).astype(I32)
    to_rows = one_hot(iota((FINE, CAP), 0) == served_row)
    a1_send[...] = pack(dot(from_rows, act[...]))

    def exchange(send, recv, ssem, rsem):
        def copy(i):
            peer = (seq + i) % N_SEQ
            return pltpu.make_async_remote_copy(
                send.at[peer], recv.at[seq], ssem.at[i], rsem.at[seq],
                device_id=(dp, peer), device_id_type=MESH)

        def start(i, carry):
            copy(i).start()
            return carry

        def wait(i, carry):
            src = (seq + i) % N_SEQ
            pltpu.make_async_remote_copy(
                send.at[src], recv.at[src], ssem.at[i], rsem.at[src],
                device_id=(dp, src), device_id_type=MESH).wait_recv()
            return carry

        def drain(i, carry):
            copy(i).wait_send()
            return carry

        return [lambda f=f: lax.fori_loop(1, N_SEQ, f, 0) for f in (start, wait, drain)]

    a1_start, a1_wait, a1_drain = exchange(a1_send, a1_recv, a1_ssem, a1_rsem)
    a2_start, a2_wait, a2_drain = exchange(a2_send, a2_recv, a2_ssem, a2_rsem)
    a1_start()
    drains.append(a1_drain)
    a1_recv[seq] = a1_send[seq]

    acts, grads = (dact, aact), (dgrad, agrad)
    ring_at = (x, y)
    first = jnp.where(core == 0, x, y)
    second = jnp.where(core == 0, y, x)
    active = first < 3

    def target(kind, p):
        if kind == 0:
            return (p * 4 + yh * 2, seq)
        return (x * 4 + (p // 2) * 2 + 1, z * 2 + p % 2)

    def act_copy(kind, p, source):
        return pltpu.make_async_remote_copy(
            acts[kind], f_act.at[source], f_ssem.at[kind * 3 + p], f_rsem.at[source],
            device_id=target(kind, p), device_id_type=MESH)

    def grad_copy(kind, p, source):
        return pltpu.make_async_remote_copy(
            grads[kind].at[:, pl.ds(p * BLOCK, BLOCK)], f_grad.at[source],
            g_ssem.at[kind * 3 + p], g_rsem.at[source],
            device_id=target(kind, p), device_id_type=MESH)

    def give_factor(kind, copy_of, keep):
        source = ring_at[kind] * 2 + core
        for p in range(3):
            mine = (core == kind) & (ring_at[kind] == p)
            when(jnp.logical_not(mine), lambda: copy_of(kind, p, source).start())
            when(mine, lambda: keep(source, p))
            drains.append(
                lambda p=p, mine=mine: when(
                    jnp.logical_not(mine), lambda: copy_of(kind, p, 0).wait_send()
                )
            )

    def give_act(kind):
        def keep(source, p):
            f_act[source] = acts[kind][...]

        give_factor(kind, act_copy, keep)

    def give_grad(kind):
        def keep(source, p):
            f_grad[source] = grads[kind][:, p * BLOCK:(p + 1) * BLOCK]

        give_factor(kind, grad_copy, keep)

    loads[2].wait()
    loads[3].wait()
    donor_act = dot(from_donor, act[...]).astype(BF16)
    donor_emb = dot(donor_act, wd[...]).astype(BF16).astype(F32)
    acceptor_emb_grad = (weighted * donor_emb * INV_ROOT).astype(BF16)
    acceptor_rows = dot_nt(acceptor_emb_grad, wa[...]).astype(BF16)
    a2_send[...] = pack(dot(to_served, acceptor_rows))
    dact[...] = donor_act
    agrad[...] = acceptor_emb_grad
    a2_start()
    give_act(0)
    give_grad(1)
    drains.append(a2_drain)
    a2_recv[seq] = a2_send[seq]

    loads[4].wait()
    other_f[pl.ds(0, COARSE)] = dot(even, other_in[...]).astype(BF16)
    other_f[pl.ds(COARSE, COARSE)] = dot(odd, other_in[...]).astype(BF16)

    a1_wait()
    acceptor_act = dot(from_served, unpack(a1_recv[...])).astype(BF16)
    acceptor_emb = dot(acceptor_act, wa[...]).astype(BF16).astype(F32)
    score = mask_column * jnp.sum(donor_emb * acceptor_emb, axis=1, keepdims=True) * INV_ROOT
    score = jnp.concatenate([score, jnp.zeros((128 - SLOTS, 1), F32)], axis=0)
    scores_out[...] = as_row(score)[:, :SLOTS]
    donor_emb_grad = (weighted * acceptor_emb * INV_ROOT).astype(BF16)
    aact[...] = acceptor_act
    dgrad[...] = donor_emb_grad

    give_grad(0)
    give_act(1)

    sources = 8

    def second_device(r):
        if_donor = x * 4 + (r // 2) * 2
        if_acceptor = r * 4 + yh * 2 + 1
        return (
            jnp.where(core == 0, if_donor, if_acceptor),
            jnp.where(core == 0, z * 2 + r % 2, seq),
        )

    def chunk_copy(r, source):
        return pltpu.make_async_remote_copy(
            sum1.at[:, r % 2, :, pl.ds((r // 2) * 128, 128)], part2.at[source],
            s2_ssem.at[r], s2_rsem.at[source], device_id=second_device(r), device_id_type=MESH)

    def z_device(zt):
        return (dp, zt * 2 + yl)

    def z_copy(i):
        zt = (z + i) % N_Z
        return pltpu.make_async_remote_copy(
            sum2.at[zt], part3.at[z], s3_ssem.at[i], s3_rsem.at[z],
            device_id=z_device(zt), device_id_type=MESH)

    tile_at = first * 2 + second // 2
    seq_to = z * 2 + second % 2

    def gather_copy(d):
        return pltpu.make_async_remote_copy(
            piece, pieces.at[core, tile_at], ag_ssem.at[d], ag_rsem.at[core, tile_at],
            device_id=(d, seq_to), device_id_type=MESH)

    def block_sum():
        for s in range(sources):
            @pl.when(s != first * 2 + core)
            def _(s=s):
                for kind in range(2):
                    @pl.when(core == kind)
                    def _(kind=kind):
                        act_copy(kind, 0, s).wait_recv()
                        grad_copy(kind, 0, s).wait_recv()

        for m in range(C_OUT // TILE):
            left = f_act[:, :, m * TILE:(m + 1) * TILE].reshape(sources * SLOTS, TILE)
            right = f_grad[...].reshape(sources * SLOTS, BLOCK)
            block = dot_tn(left, right).astype(BF16)
            for g in range(TILE // 16):
                row = m * TILE + g * 16
                s, at_row = row // ROWS_SEQ, row % ROWS_SEQ
                sum1[s // 2, s % 2, at_row:at_row + 16, :] = block[g * 16:(g + 1) * 16]
        for r in range(4):
            when(r != second, lambda: chunk_copy(r, second).start())

            @pl.when(r == second)
            def _(r=r):
                part2[r] = sum1[:, r % 2, :, (r // 2) * 128:(r // 2) * 128 + 128]

    def block_drain():
        for r in range(4):
            when(r != second, lambda: chunk_copy(r, second).wait_send())

    def ring_sum():
        for r in range(4):
            when(r != second, lambda: chunk_copy(r, r).wait_recv())
        sum2[...] = (
            part2[0].astype(F32) + part2[1].astype(F32) + part2[2].astype(F32) + part2[3].astype(F32)
        ).astype(BF16)
        for i in range(1, N_Z):
            z_copy(i).start()
        part3[z] = sum2[z]

    def ring_drain():
        for i in range(1, N_Z):
            z_copy(i).wait_send()

    def z_sum():
        for i in range(1, N_Z):
            src = (z + i) % N_Z
            pltpu.make_async_remote_copy(
                sum2.at[src], part3.at[src], s3_ssem.at[i], s3_rsem.at[src],
                device_id=z_device(src), device_id_type=MESH).wait_recv()
        total = part3[0].astype(F32)
        for i in range(1, N_Z):
            total = total + part3[i].astype(F32)
        piece[...] = (total * (1.0 / N_DP)).astype(BF16)
        for d in range(N_DP):
            mine = (d == dp) & (seq_to == seq)
            when(jnp.logical_not(mine), lambda: gather_copy(d).start())

            @pl.when(mine)
            def _(d=d):
                pieces[core, tile_at] = piece[...]

    def z_drain():
        for d in range(N_DP):
            when(jnp.logical_not((d == dp) & (seq_to == seq)), lambda: gather_copy(d).wait_send())

    donor_rows = dot_nt(donor_emb_grad, wd[...]).astype(BF16)
    a2_wait()
    served_rows = unpack(a2_recv[...])

    def grad_of(rows):
        total = (
            other_f[rows].astype(F32)
            + dot(to_rows[rows.start:rows.start + rows.size], served_rows)
            + dot(to_donor[rows.start:rows.start + rows.size, :SLOTS], donor_rows)
        )
        return total * slope[rows]

    g_even = grad_of(pl.ds(0, COARSE))
    g_odd = grad_of(pl.ds(COARSE, COARSE))
    pair = g_even + g_odd
    pe[pl.ds(0, COARSE)] = pair.astype(BF16)
    grad_left[pl.ds(0, 16)] = pair[:16].astype(BF16)
    grad_left[pl.ds(16, 16)] = g_even[:16].astype(BF16)
    grad_right[pl.ds(0, 16)] = pair[COARSE - 16:].astype(BF16)
    grad_right[pl.ds(16, 16)] = g_odd[COARSE - 16:].astype(BF16)

    def ghalo_left():
        return pltpu.make_async_remote_copy(
            grad_left, grad_next, ghalo_ssem.at[0], ghalo_rsem.at[0],
            device_id=(dp, (seq + N_SEQ - 1) % N_SEQ), device_id_type=MESH)

    def ghalo_right():
        return pltpu.make_async_remote_copy(
            grad_right, grad_prev, ghalo_ssem.at[1], ghalo_rsem.at[1],
            device_id=(dp, (seq + 1) % N_SEQ), device_id_type=MESH)

    when(seq > 0, lambda: ghalo_left().start())
    when(seq < N_SEQ - 1, lambda: ghalo_right().start())
    drains.append(lambda: when(seq > 0, lambda: ghalo_left().wait_send()))
    drains.append(lambda: when(seq < N_SEQ - 1, lambda: ghalo_right().wait_send()))

    shifted = pltpu.roll(g_odd, 1, 0)
    po[pl.ds(0, COARSE)] = (shifted + g_even).astype(BF16)

    when(active, block_sum)
    drains.append(lambda: when(active, block_drain))

    when(seq < N_SEQ - 1, lambda: ghalo_left().wait_recv())
    when(seq > 0, lambda: ghalo_right().wait_recv())

    grow = iota((16, C_OUT), 0)
    after = grad_next[...].astype(F32)
    prior = grad_prev[...].astype(F32)
    pe[pl.ds(COARSE, 16)] = jnp.where(
        grow == 0, after[:16], jnp.where(grow == 15, prior[:16], 0.0)
    ).astype(BF16)
    prior_odd = pltpu.roll(prior[16:], 1, 0)
    po[pl.ds(0, 16)] = (
        jnp.where(grow == 0, prior_odd, shifted[:16]) + g_even[:16]
    ).astype(BF16)
    last_odd = pltpu.roll(g_odd[COARSE - 16:], 1, 0)
    po[pl.ds(COARSE, 16)] = jnp.where(grow == 0, last_odd + after[16:], 0.0).astype(BF16)

    def back_tile(n, carry):
        cols = pl.ds(pl.multiple_of(n * TILE, TILE), TILE)
        pairs, cross = pe[...], po[...]
        ahead = dot_nt(pairs, w[0, cols, :]) + dot_nt(cross, w[1, cols, :])
        here = dot_nt(pairs[:COARSE], w[2, cols, :]) + dot_nt(cross[:COARSE], w[3, cols, :])
        behind = dot_nt(pairs, w[4, cols, :])
        total = here + pltpu.roll(ahead, EXT - 1, 0)[:COARSE] + pltpu.roll(behind, 1, 0)[:COARSE]
        coarse_out[0, :, cols] = total.astype(BF16)
        return carry

    lax.fori_loop(0, C_IN // TILE, back_tile, 0)
    when(active, ring_sum)
    drains.append(lambda: when(active, ring_drain))

    when(active, z_sum)
    drains.append(lambda: when(active, z_drain))

    for kind, out in ((0, donor_out), (1, acceptor_out)):
        for t in range(6):
            if kind == 0:
                source = ((t // 2) * 4 + (t % 2) * 2, seq)
            else:
                y_s = t // 2
                source = (((t % 2) * 2 + yl) * 4 + (y_s // 2) * 2 + 1, z * 2 + y_s % 2)
            mine = (source[0] == dp) & (source[1] == seq)

            @pl.when(jnp.logical_not(mine))
            def _(kind=kind, t=t, source=source):
                pltpu.make_async_remote_copy(
                    piece, pieces.at[kind, t], ag_ssem.at[0], ag_rsem.at[kind, t],
                    device_id=source, device_id_type=MESH).wait_recv()

            out[:, t * 128:(t + 1) * 128] = pieces[kind, t].astype(F32)

    finish()


def write_out(*refs):
    sem = refs[8]
    copies = [pltpu.make_async_copy(refs[i], refs[4 + i], sem.at[i]) for i in range(4)]
    for copy in copies:
        copy.start()
    for copy in copies:
        copy.wait()


def on_device(*args):
    vmem = pl.BlockSpec(memory_space=pltpu.VMEM)
    hbm = pl.BlockSpec(memory_space=pltpu.HBM)
    dma = pltpu.SemaphoreType.DMA

    def v(*shape, dtype=BF16):
        return pltpu.VMEM(shape, dtype)

    scratch = [
        v(1, SLOTS, dtype=F32), v(1, SLOTS, dtype=I32), v(1, SLOTS, dtype=I32), v(1, SLOTS, dtype=I32),
        v(TAPS, C_IN, C_OUT), v(C_OUT, EMB), v(C_OUT, EMB), v(EXT, C_IN),
        v(FINE, C_OUT), v(FINE, C_OUT), v(FINE, C_OUT), v(FINE, C_OUT),
        v(FINE, C_OUT), v(FINE, C_OUT, dtype=F32),
        v(16, C_IN), v(16, C_IN), v(32, C_OUT), v(32, C_OUT), v(32, C_OUT), v(32, C_OUT),
        v(8, 128, dtype=I32), v(N_SEQ, 8, 128, dtype=I32),
        v(N_SEQ, 16, HALF), v(N_SEQ, 16, HALF), v(N_SEQ, 16, HALF), v(N_SEQ, 16, HALF),
        v(EXT, C_OUT), v(EXT, C_OUT),
        v(SLOTS, C_OUT), v(SLOTS, EMB), v(SLOTS, C_OUT), v(SLOTS, EMB),
        v(8, SLOTS, C_OUT), v(8, SLOTS, BLOCK), v(N_Z, 2, ROWS_SEQ, BLOCK),
        v(4, N_Z, ROWS_SEQ, 128), v(N_Z, ROWS_SEQ, 128), v(N_Z, ROWS_SEQ, 128),
        v(ROWS_SEQ, 128), v(2, 6, ROWS_SEQ, 128),
        dma((9,)), dma((3,)), dma((2,)), dma((2,)), dma((2,)), dma((2,)),
        dma((N_SEQ,)), dma((N_SEQ,)), dma((N_SEQ,)), dma((N_SEQ,)), dma((N_SEQ,)), dma((N_SEQ,)),
        dma((6,)), dma((8,)), dma((6,)), dma((8,)),
        dma((4,)), dma((4,)), dma((N_Z,)), dma((N_Z,)), dma((N_DP,)), dma((2, 6)),
    ]
    shapes = (
        jax.ShapeDtypeStruct((1, SLOTS), F32),
        jax.ShapeDtypeStruct((1, COARSE, C_IN), BF16),
        jax.ShapeDtypeStruct((ROWS_SEQ, EMB), F32),
        jax.ShapeDtypeStruct((ROWS_SEQ, EMB), F32),
    )
    args = [pltpu.with_memory_space_constraint(a, pltpu.HBM) for a in args]
    results = pl.pallas_call(
        kernel,
        out_shape=shapes,
        in_specs=[hbm] * 10,
        out_specs=(vmem,) * 4,
        scratch_shapes=scratch,
        compiler_params=pltpu.CompilerParams(
            collective_id=0, has_side_effects=True, vmem_limit_bytes=48*1024*1024
        ),
    )(*args)
    return pl.pallas_call(
        write_out,
        out_shape=shapes,
        in_specs=[vmem] * 4,
        out_specs=(pl.BlockSpec(memory_space=pl.ANY),) * 4,
        scratch_shapes=[dma((4,))],
        compiler_params=pltpu.CompilerParams(vmem_limit_bytes=1024 * 1024),
    )(*results)


def solution(mesh):
    rows, slots = P("dp", "seq", None), P("dp", "seq")
    return jax.shard_map(
        on_device,
        mesh=mesh,
        in_specs=(rows, rows, P(), P(), P(), rows, slots, slots, slots, slots),
        out_specs=(slots, rows, P("seq", None), P("seq", None)),
        check_vma=False,
    )
```

time: 68.3 us -> 53 us (0.78)
  local copies, waits for them, and re-layouts: 11.1 us -> 0 us
  Pallas kernels: 56.3 us -> 52.2 us
    unnamed x22 -> x0, local copies, waits for them, and re-layouts: 11.1 us -> none
    pallas_call x1 -> x2, Pallas kernels: 56.3 us -> 52.2 us  [the longest x1 51.3 us: on_device(): pl.pallas_call(kernel, out_shape=shapes, in_specs=[hbm] * 10, out_specs=(...]
where the time goes in v2:
time: 53 us; the launch traced here: 52.9 us
  Pallas kernels  52.2 us (98%)
  between operations  0.64 us (1%)
    pallas_call x1, Pallas kernels, on_device(): pl.pallas_call(kernel, out_shape=shapes, in_specs=[hbm] * 10, out_specs=(...  51.3 us

profile of v2, /device:TPU:1, one launch (start us, length us, event | category | flops | bytes accessed | tf_op | source)
XLA Modules:
  0.0 52.9 jit_solution(11892134557303929558)
XLA Ops:
  0.6 51.3 %shard_map.129 = (f32[1,64]{1,0:T(1,128)S(1)}, bf16[1,256,1024]{2,1,0:T(8,128)(2,1)S(1)}, f32[48,768]{1,0:T(8,128)S(1)}, f32[48,768]{1,0:T(8,128)S(1)}) custom-call(bf16[1,256,1024]{2,1,0:T(8,128)(2,1)} %coarse.1, bf16[1,512,768]{2,1,0:T(8,128)(2,1)} %skip.1, bf16[5,1024,768]{2,1,0:T(8,128)(2,1)} %conv_w.1, bf16[768,768]{1,0:T(8,128)(2,1)} %donor_w.1, ...), custom_call_target="tpu_custom_call" | custom-call | tf_op jit(solution)/shard_map/pallas_call | solution.py:601
  52.0 0.9 %shard_map.130 = (f32[1,64]{1,0:T(1,128)}, bf16[1,256,1024]{2,1,0:T(8,128)(2,1)}, f32[48,768]{1,0:T(8,128)}, f32[48,768]{1,0:T(8,128)}) custom-call(f32[1,64]{1,0:T(1,128)S(1)} %get-tuple-element.8.refs_0_, bf16[1,256,1024]{2,1,0:T(8,128)(2,1)S(1)} %get-tuple-element.9.refs_1_, f32[48,768]{1,0:T(8,128)S(1)} %get-tuple-element.10.refs_2_, ...), custom_call_target="tpu_custom_call" | custom-call | tf_op jit(solution)/shard_map/pallas_call | solution.py:611

commit v3 on v2

--- a/solution.py
+++ b/solution.py
@@ -17,6 +17,7 @@
 CAP = N_SEQ * ACAP
 TILE = 256
 HALF = 384
+BLOCKS = (((1, 2), (0, 0), (0, 1)), ((1, 0), (0, 2), (1, 1)))
 BLOCK = 256
 ROWS_SEQ = C_OUT // N_SEQ
 INV_ROOT = 1.0 / math.sqrt(EMB)
@@ -74,7 +75,7 @@
     halo_next, halo_prev, grad_next, grad_prev, grad_left, grad_right,
     pos_own, pos_all, a1_send, a1_recv, a2_send, a2_recv,
     pe, po, dact, dgrad, aact, agrad,
-    f_act, f_grad, sum1, part2, sum2, part3, piece, pieces,
+    f_act, f_grad, sum1, act_t, part2, sum2, part3, piece, pieces,
     load_sem, w_sem, halo_ssem, halo_rsem, ghalo_ssem, ghalo_rsem,
     pos_ssem, pos_rsem, a1_ssem, a1_rsem, a2_ssem, a2_rsem,
     f_ssem, f_rsem, g_ssem, g_rsem,
@@ -121,20 +122,20 @@
     grad_prev[...] = jnp.zeros_like(grad_prev)
     barrier = pltpu.get_barrier_semaphore()
 
-    def greet_seq(i, carry):
+    def greet_seq(i):
         pl.semaphore_signal(barrier, inc=1, device_id=(dp, (seq + i) % N_SEQ), device_id_type=MESH)
-        return carry
-
-    def greet_dp(i, carry):
+
+    def greet_dp(i):
         other_dp = (dp + i) % N_DP
         pl.semaphore_signal(barrier, inc=1, device_id=(other_dp, seq), device_id_type=MESH)
         pl.semaphore_signal(
             barrier, inc=1, device_id=(other_dp, z * 2 + 1 - yl), device_id_type=MESH
         )
-        return carry
-
-    lax.fori_loop(1, N_SEQ, greet_seq, 0)
-    lax.fori_loop(1, N_DP, greet_dp, 0)
+
+    for i in range(1, N_SEQ):
+        greet_seq(i)
+    for i in range(1, N_DP):
+        greet_dp(i)
     load_w(0).start()
     loads[1].start()
     for n in range(1, C_OUT // TILE):
@@ -292,43 +293,48 @@
     second = jnp.where(core == 0, y, x)
     active = first < 3
 
-    def target(kind, p):
-        if kind == 0:
+    def target(ring, p):
+        if ring == 0:
             return (p * 4 + yh * 2, seq)
         return (x * 4 + (p // 2) * 2 + 1, z * 2 + p % 2)
 
-    def act_copy(kind, p, source):
-        return pltpu.make_async_remote_copy(
-            acts[kind], f_act.at[source], f_ssem.at[kind * 3 + p], f_rsem.at[source],
-            device_id=target(kind, p), device_id_type=MESH)
-
-    def grad_copy(kind, p, source):
-        return pltpu.make_async_remote_copy(
-            grads[kind].at[:, pl.ds(p * BLOCK, BLOCK)], f_grad.at[source],
-            g_ssem.at[kind * 3 + p], g_rsem.at[source],
-            device_id=target(kind, p), device_id_type=MESH)
+    def act_copy(ring, p, source):
+        kind = BLOCKS[ring][p][0]
+        return pltpu.make_async_remote_copy(
+            acts[kind], f_act.at[source], f_ssem.at[ring * 3 + p], f_rsem.at[source],
+            device_id=target(ring, p), device_id_type=MESH)
+
+    def grad_copy(ring, p, source):
+        kind, block = BLOCKS[ring][p]
+        return pltpu.make_async_remote_copy(
+            grads[kind].at[:, pl.ds(block * BLOCK, BLOCK)], f_grad.at[source],
+            g_ssem.at[ring * 3 + p], g_rsem.at[source],
+            device_id=target(ring, p), device_id_type=MESH)
 
     def give_factor(kind, copy_of, keep):
-        source = ring_at[kind] * 2 + core
-        for p in range(3):
-            mine = (core == kind) & (ring_at[kind] == p)
-            when(jnp.logical_not(mine), lambda: copy_of(kind, p, source).start())
-            when(mine, lambda: keep(source, p))
-            drains.append(
-                lambda p=p, mine=mine: when(
-                    jnp.logical_not(mine), lambda: copy_of(kind, p, 0).wait_send()
+        for ring in range(2):
+            source = ring_at[ring] * 2 + core
+            for p in range(3):
+                if BLOCKS[ring][p][0] != kind:
+                    continue
+                mine = (core == ring) & (ring_at[ring] == p)
+                when(jnp.logical_not(mine), lambda: copy_of(ring, p, source).start())
+                when(mine, lambda: keep(source, BLOCKS[ring][p][1]))
+                drains.append(
+                    lambda ring=ring, p=p, mine=mine: when(
+                        jnp.logical_not(mine), lambda: copy_of(ring, p, 0).wait_send()
+                    )
                 )
-            )
 
     def give_act(kind):
-        def keep(source, p):
+        def keep(source, block):
             f_act[source] = acts[kind][...]
 
         give_factor(kind, act_copy, keep)
 
     def give_grad(kind):
-        def keep(source, p):
-            f_grad[source] = grads[kind][:, p * BLOCK:(p + 1) * BLOCK]
+        def keep(source, block):
+            f_grad[source] = grads[kind][:, block * BLOCK:(block + 1) * BLOCK]
 
         give_factor(kind, grad_copy, keep)
 
@@ -341,11 +347,8 @@
     a2_send[...] = pack(dot(to_served, acceptor_rows))
     dact[...] = donor_act
     agrad[...] = acceptor_emb_grad
-    a2_start()
     give_act(0)
     give_grad(1)
-    drains.append(a2_drain)
-    a2_recv[seq] = a2_send[seq]
 
     loads[4].wait()
     other_f[pl.ds(0, COARSE)] = dot(even, other_in[...]).astype(BF16)
@@ -353,16 +356,18 @@
 
     a1_wait()
     acceptor_act = dot(from_served, unpack(a1_recv[...])).astype(BF16)
+    aact[...] = acceptor_act
+    give_act(1)
     acceptor_emb = dot(acceptor_act, wa[...]).astype(BF16).astype(F32)
     score = mask_column * jnp.sum(donor_emb * acceptor_emb, axis=1, keepdims=True) * INV_ROOT
     score = jnp.concatenate([score, jnp.zeros((128 - SLOTS, 1), F32)], axis=0)
     scores_out[...] = as_row(score)[:, :SLOTS]
     donor_emb_grad = (weighted * acceptor_emb * INV_ROOT).astype(BF16)
-    aact[...] = acceptor_act
     dgrad[...] = donor_emb_grad
-
     give_grad(0)
-    give_act(1)
+    a2_start()
+    drains.append(a2_drain)
+    a2_recv[seq] = a2_send[seq]
 
     sources = 8
 
@@ -376,7 +381,7 @@
 
     def chunk_copy(r, source):
         return pltpu.make_async_remote_copy(
-            sum1.at[:, r % 2, :, pl.ds((r // 2) * 128, 128)], part2.at[source],
+            sum1.at[r // 2, :, r % 2], part2.at[source],
             s2_ssem.at[r], s2_rsem.at[source], device_id=second_device(r), device_id_type=MESH)
 
     def z_device(zt):
@@ -388,38 +393,40 @@
             sum2.at[zt], part3.at[z], s3_ssem.at[i], s3_rsem.at[z],
             device_id=z_device(zt), device_id_type=MESH)
 
-    tile_at = first * 2 + second // 2
+    def of_block(i):
+        value = 0
+        for ring in range(2):
+            for p in range(3):
+                hit = (core == ring) & (first == p)
+                value = jnp.where(hit, BLOCKS[ring][p][i], value)
+        return value
+
+    kind_at = of_block(0)
+    tile_at = of_block(1) * 2 + second // 2
     seq_to = z * 2 + second % 2
 
     def gather_copy(d):
         return pltpu.make_async_remote_copy(
-            piece, pieces.at[core, tile_at], ag_ssem.at[d], ag_rsem.at[core, tile_at],
+            piece, pieces.at[kind_at, tile_at], ag_ssem.at[d], ag_rsem.at[kind_at, tile_at],
             device_id=(d, seq_to), device_id_type=MESH)
 
     def block_sum():
         for s in range(sources):
-            @pl.when(s != first * 2 + core)
-            def _(s=s):
-                for kind in range(2):
-                    @pl.when(core == kind)
-                    def _(kind=kind):
-                        act_copy(kind, 0, s).wait_recv()
-                        grad_copy(kind, 0, s).wait_recv()
-
-        for m in range(C_OUT // TILE):
-            left = f_act[:, :, m * TILE:(m + 1) * TILE].reshape(sources * SLOTS, TILE)
-            right = f_grad[...].reshape(sources * SLOTS, BLOCK)
-            block = dot_tn(left, right).astype(BF16)
-            for g in range(TILE // 16):
-                row = m * TILE + g * 16
-                s, at_row = row // ROWS_SEQ, row % ROWS_SEQ
-                sum1[s // 2, s % 2, at_row:at_row + 16, :] = block[g * 16:(g + 1) * 16]
-        for r in range(4):
-            when(r != second, lambda: chunk_copy(r, second).start())
-
-            @pl.when(r == second)
-            def _(r=r):
-                part2[r] = sum1[:, r % 2, :, (r // 2) * 128:(r // 2) * 128 + 128]
+            when(s != first * 2 + core, lambda: act_copy(0, 0, s).wait_recv())
+        act_t[...] = jnp.transpose(f_act[...].reshape(sources * SLOTS, C_OUT))
+        for s in range(sources):
+            when(s != first * 2 + core, lambda: grad_copy(0, 0, s).wait_recv())
+        for t in range(2):
+            right = f_grad[:, :, t * 128:(t + 1) * 128].reshape(sources * SLOTS, 128)
+            for m in range(2):
+                block = dot(act_t[m * HALF:(m + 1) * HALF, :], right).astype(BF16)
+                sum1[t, m * 4:(m + 1) * 4] = block.reshape(4, 2, ROWS_SEQ, 128)
+            for r in (2 * t, 2 * t + 1):
+                when(r != second, lambda: chunk_copy(r, second).start())
+
+                @pl.when(r == second)
+                def _(r=r):
+                    part2[r] = sum1[r // 2, :, r % 2]
 
     def block_drain():
         for r in range(4):
@@ -455,13 +462,16 @@
 
             @pl.when(mine)
             def _(d=d):
-                pieces[core, tile_at] = piece[...]
+                pieces[kind_at, tile_at] = piece[...]
 
     def z_drain():
         for d in range(N_DP):
             when(jnp.logical_not((d == dp) & (seq_to == seq)), lambda: gather_copy(d).wait_send())
 
     donor_rows = dot_nt(donor_emb_grad, wd[...]).astype(BF16)
+    when(active, block_sum)
+    drains.append(lambda: when(active, block_drain))
+
     a2_wait()
     served_rows = unpack(a2_recv[...])
 
@@ -499,9 +509,6 @@
 
     shifted = pltpu.roll(g_odd, 1, 0)
     po[pl.ds(0, COARSE)] = (shifted + g_even).astype(BF16)
-
-    when(active, block_sum)
-    drains.append(lambda: when(active, block_drain))
 
     when(seq < N_SEQ - 1, lambda: ghalo_left().wait_recv())
     when(seq > 0, lambda: ghalo_right().wait_recv())
@@ -519,6 +526,9 @@
     last_odd = pltpu.roll(g_odd[COARSE - 16:], 1, 0)
     po[pl.ds(COARSE, 16)] = jnp.where(grow == 0, last_odd + after[16:], 0.0).astype(BF16)
 
+    when(active, ring_sum)
+    drains.append(lambda: when(active, ring_drain))
+
     def back_tile(n, carry):
         cols = pl.ds(pl.multiple_of(n * TILE, TILE), TILE)
         pairs, cross = pe[...], po[...]
@@ -530,19 +540,17 @@
         return carry
 
     lax.fori_loop(0, C_IN // TILE, back_tile, 0)
-    when(active, ring_sum)
-    drains.append(lambda: when(active, ring_drain))
-
     when(active, z_sum)
     drains.append(lambda: when(active, z_drain))
 
     for kind, out in ((0, donor_out), (1, acceptor_out)):
         for t in range(6):
-            if kind == 0:
-                source = ((t // 2) * 4 + (t % 2) * 2, seq)
+            ring = 0 if (kind, t // 2) in BLOCKS[0] else 1
+            p = BLOCKS[ring].index((kind, t // 2))
+            if ring == 0:
+                source = (p * 4 + (t % 2) * 2, seq)
             else:
-                y_s = t // 2
-                source = (((t % 2) * 2 + yl) * 4 + (y_s // 2) * 2 + 1, z * 2 + y_s % 2)
+                source = (((t % 2) * 2 + yl) * 4 + (p // 2) * 2 + 1, z * 2 + p % 2)
             mine = (source[0] == dp) & (source[1] == seq)
 
             @pl.when(jnp.logical_not(mine))
@@ -583,7 +591,7 @@
         v(N_SEQ, 16, HALF), v(N_SEQ, 16, HALF), v(N_SEQ, 16, HALF), v(N_SEQ, 16, HALF),
         v(EXT, C_OUT), v(EXT, C_OUT),
         v(SLOTS, C_OUT), v(SLOTS, EMB), v(SLOTS, C_OUT), v(SLOTS, EMB),
-        v(8, SLOTS, C_OUT), v(8, SLOTS, BLOCK), v(N_Z, 2, ROWS_SEQ, BLOCK),
+        v(8, SLOTS, C_OUT), v(8, SLOTS, BLOCK), v(2, N_Z, 2, ROWS_SEQ, 128), v(C_OUT, 8 * SLOTS),
         v(4, N_Z, ROWS_SEQ, 128), v(N_Z, ROWS_SEQ, 128), v(N_Z, ROWS_SEQ, 128),
         v(ROWS_SEQ, 128), v(2, 6, ROWS_SEQ, 128),
         dma((9,)), dma((3,)), dma((2,)), dma((2,)), dma((2,)), dma((2,)),

time: 53 us -> 51.6 us (0.974)
  Pallas kernels: 52.2 us -> 50.9 us
    pallas_call x1, Pallas kernels: 51.3 us -> 50 us  [on_device(): pl.pallas_call(kernel, out_shape=shapes, in_specs=[hbm] * 10, out_specs=(...]
where the time goes in v3:
time: 51.6 us; the launch traced here: 51.5 us
  Pallas kernels  50.9 us (99%)
  between operations  0.64 us (1%)
    pallas_call x1, Pallas kernels, on_device(): pl.pallas_call(kernel, out_shape=shapes, in_specs=[hbm] * 10, out_specs=(...  50 us

profile of v3, /device:TPU:1, one launch (start us, length us, event | category | flops | bytes accessed | tf_op | source)
XLA Modules:
  0.0 51.5 jit_solution(10514397432752285367)
XLA Ops:
  0.6 50.0 %shard_map.129 = (f32[1,64]{1,0:T(1,128)S(1)}, bf16[1,256,1024]{2,1,0:T(8,128)(2,1)S(1)}, f32[48,768]{1,0:T(8,128)S(1)}, f32[48,768]{1,0:T(8,128)S(1)}) custom-call(bf16[1,256,1024]{2,1,0:T(8,128)(2,1)} %coarse.1, bf16[1,512,768]{2,1,0:T(8,128)(2,1)} %skip.1, bf16[5,1024,768]{2,1,0:T(8,128)(2,1)} %conv_w.1, bf16[768,768]{1,0:T(8,128)(2,1)} %donor_w.1, ...), custom_call_target="tpu_custom_call" | custom-call | tf_op jit(solution)/shard_map/pallas_call | solution.py:609
  50.6 0.9 %shard_map.130 = (f32[1,64]{1,0:T(1,128)}, bf16[1,256,1024]{2,1,0:T(8,128)(2,1)}, f32[48,768]{1,0:T(8,128)}, f32[48,768]{1,0:T(8,128)}) custom-call(f32[1,64]{1,0:T(1,128)S(1)} %get-tuple-element.8.refs_0_, bf16[1,256,1024]{2,1,0:T(8,128)(2,1)S(1)} %get-tuple-element.9.refs_1_, f32[48,768]{1,0:T(8,128)S(1)} %get-tuple-element.10.refs_2_, ...), custom_call_target="tpu_custom_call" | custom-call | tf_op jit(solution)/shard_map/pallas_call | solution.py:619

commit v4 on v3

--- a/solution.py
+++ b/solution.py
@@ -18,6 +18,11 @@
 TILE = 256
 HALF = 384
 BLOCKS = (((1, 2), (0, 0), (0, 1)), ((1, 0), (0, 2), (1, 1)))
+FAR_SEQ = (8, 7, 9, 6, 10, 5, 11, 4, 12, 3, 13, 2, 14, 1, 15)
+FAR_Z = (4, 3, 5, 2, 6, 1, 7)
+FAR_DP = tuple(
+    (dx, dy, dc) for dx, dy in ((2, 1), (2, 0), (1, 1), (3, 1), (0, 1), (1, 0), (3, 0)) for dc in (0, 1)
+) + ((0, 0, 1),)
 BLOCK = 256
 ROWS_SEQ = C_OUT // N_SEQ
 INV_ROOT = 1.0 / math.sqrt(EMB)
@@ -170,11 +175,8 @@
             pos_own, pos_all.at[seq], pos_ssem.at[i], pos_rsem.at[seq],
             device_id=(dp, (seq + i) % N_SEQ), device_id_type=MESH)
 
-    def pos_start(i, carry):
+    for i in FAR_SEQ:
         pos_copy(i).start()
-        return carry
-
-    lax.fori_loop(1, N_SEQ, pos_start, 0)
     drains.append(
         lambda: lax.fori_loop(1, N_SEQ, lambda i, carry: (pos_copy(i).wait_send(), carry)[1], 0)
     )
@@ -264,9 +266,9 @@
                 send.at[peer], recv.at[seq], ssem.at[i], rsem.at[seq],
                 device_id=(dp, peer), device_id_type=MESH)
 
-        def start(i, carry):
-            copy(i).start()
-            return carry
+        def start():
+            for i in FAR_SEQ:
+                copy(i).start()
 
         def wait(i, carry):
             src = (seq + i) % N_SEQ
@@ -279,7 +281,7 @@
             copy(i).wait_send()
             return carry
 
-        return [lambda f=f: lax.fori_loop(1, N_SEQ, f, 0) for f in (start, wait, drain)]
+        return [start] + [lambda f=f: lax.fori_loop(1, N_SEQ, f, 0) for f in (wait, drain)]
 
     a1_start, a1_wait, a1_drain = exchange(a1_send, a1_recv, a1_ssem, a1_rsem)
     a2_start, a2_wait, a2_drain = exchange(a2_send, a2_recv, a2_ssem, a2_rsem)
@@ -405,6 +407,9 @@
     tile_at = of_block(1) * 2 + second // 2
     seq_to = z * 2 + second % 2
 
+    def dp_at(dx, dy, dc):
+        return ((x + dx) % N_X) * 4 + ((yh + dy) % 2) * 2 + (core + dc) % 2
+
     def gather_copy(d):
         return pltpu.make_async_remote_copy(
             piece, pieces.at[kind_at, tile_at], ag_ssem.at[d], ag_rsem.at[kind_at, tile_at],
@@ -438,7 +443,7 @@
         sum2[...] = (
             part2[0].astype(F32) + part2[1].astype(F32) + part2[2].astype(F32) + part2[3].astype(F32)
         ).astype(BF16)
-        for i in range(1, N_Z):
+        for i in FAR_Z:
             z_copy(i).start()
         part3[z] = sum2[z]
 
@@ -456,17 +461,18 @@
         for i in range(1, N_Z):
             total = total + part3[i].astype(F32)
         piece[...] = (total * (1.0 / N_DP)).astype(BF16)
-        for d in range(N_DP):
-            mine = (d == dp) & (seq_to == seq)
-            when(jnp.logical_not(mine), lambda: gather_copy(d).start())
-
-            @pl.when(mine)
-            def _(d=d):
-                pieces[kind_at, tile_at] = piece[...]
+        for offset in FAR_DP:
+            gather_copy(dp_at(*offset)).start()
+        when(seq_to != seq, lambda: gather_copy(dp).start())
+
+        @pl.when(seq_to == seq)
+        def _():
+            pieces[kind_at, tile_at] = piece[...]
 
     def z_drain():
-        for d in range(N_DP):
-            when(jnp.logical_not((d == dp) & (seq_to == seq)), lambda: gather_copy(d).wait_send())
+        for offset in FAR_DP:
+            gather_copy(dp_at(*offset)).wait_send()
+        when(seq_to != seq, lambda: gather_copy(dp).wait_send())
 
     donor_rows = dot_nt(donor_emb_grad, wd[...]).astype(BF16)
     when(active, block_sum)
@@ -541,7 +547,7 @@
 
     lax.fori_loop(0, C_IN // TILE, back_tile, 0)
     when(active, z_sum)
-    drains.append(lambda: when(active, z_drain))
+    finish()
 
     for kind, out in ((0, donor_out), (1, acceptor_out)):
         for t in range(6):
@@ -561,7 +567,7 @@
 
             out[:, t * 128:(t + 1) * 128] = pieces[kind, t].astype(F32)
 
-    finish()
+    when(active, z_drain)
 
 
 def write_out(*refs):

time: 51.6 us -> 50.6 us (0.981)
  Pallas kernels: 50.9 us -> 49.8 us
    pallas_call x1, Pallas kernels: 50 us -> 48.9 us  [on_device(): pl.pallas_call(kernel, out_shape=shapes, in_specs=[hbm] * 10, out_specs=(...]
where the time goes in v4:
time: 50.6 us; the launch traced here: 50.5 us
  Pallas kernels  49.8 us (98%)
  between operations  0.64 us (1%)
    pallas_call x1, Pallas kernels, on_device(): pl.pallas_call(kernel, out_shape=shapes, in_specs=[hbm] * 10, out_specs=(...  48.9 us

profile of v4, /device:TPU:1, one launch (start us, length us, event | category | flops | bytes accessed | tf_op | source)
XLA Modules:
  0.0 50.5 jit_solution(15335456039294856107)
XLA Ops:
  0.6 48.9 %shard_map.129 = (f32[1,64]{1,0:T(1,128)S(1)}, bf16[1,256,1024]{2,1,0:T(8,128)(2,1)S(1)}, f32[48,768]{1,0:T(8,128)S(1)}, f32[48,768]{1,0:T(8,128)S(1)}) custom-call(bf16[1,256,1024]{2,1,0:T(8,128)(2,1)} %coarse.1, bf16[1,512,768]{2,1,0:T(8,128)(2,1)} %skip.1, bf16[5,1024,768]{2,1,0:T(8,128)(2,1)} %conv_w.1, bf16[768,768]{1,0:T(8,128)(2,1)} %donor_w.1, ...), custom_call_target="tpu_custom_call" | custom-call | tf_op jit(solution)/shard_map/pallas_call | solution.py:615
  49.6 0.9 %shard_map.130 = (f32[1,64]{1,0:T(1,128)}, bf16[1,256,1024]{2,1,0:T(8,128)(2,1)}, f32[48,768]{1,0:T(8,128)}, f32[48,768]{1,0:T(8,128)}) custom-call(f32[1,64]{1,0:T(1,128)S(1)} %get-tuple-element.8.refs_0_, bf16[1,256,1024]{2,1,0:T(8,128)(2,1)S(1)} %get-tuple-element.9.refs_1_, f32[48,768]{1,0:T(8,128)S(1)} %get-tuple-element.10.refs_2_, ...), custom_call_target="tpu_custom_call" | custom-call | tf_op jit(solution)/shard_map/pallas_call | solution.py:625
